TPU v7x, 128 devices: a whole 4x4x4 slice. The times are simulated.
128 devices in a mesh: crow: 8 (over x, z_hi), ccol: 4 (over z_lo, core), band: 4 (over y).
Axes of the slice: x: 4, y: 4, z: 4 (z_hi: 2, z_lo: 2; z = z_hi * 2 + z_lo), core: 2. Of those that a mesh axis runs over, the one named last changes fastest.
Arguments:
- light_field: bfloat16 [4, 16, 16, 64, 4096], P(None, 'crow', 'ccol', 'band'), may hold values from -6 to 6
- channel_weights: float32 [4], replicated, may hold values from 0.2 to 1
Outputs:
- depth: float32 [16, 16, 64, 4096], P('crow', 'ccol', 'band')
All inputs are finite; a program needn't handle non-finite values.
Results may differ from a plain program's by a relative error of at most 0.0043.
Values may be sent and summed in bfloat16 or wider, within the bound.
No kernel may reach another device: no remote copies, remote signals or barrier semaphores. Data moves between devices by JAX's collectives and lax.ppermute only.
A program may use at most 128 MiB of HBM per device.

v0:
```python
import functools

import jax
import jax.numpy as jnp
from jax import lax
from jax.experimental import pallas as pl
from jax.experimental.pallas import tpu as pltpu
from jax.sharding import PartitionSpec as P

F32, BF16 = jnp.float32, jnp.bfloat16
LANES = 128
MIB = 1 << 20
NT = (((1,), (1,)), ((), ()))


def iota(shape, dim):
    return lax.broadcasted_iota(jnp.int32, shape, dim)


def ones_where(*conditions_and_values):
    total = None
    for condition, value in conditions_and_values:
        term = jnp.where(condition, F32(value), F32(0.0))
        total = term if total is None else total + term
    return total


def gray_kernel(chunks, weights_ref, field_ref, out_ref, field, arrived):
    copies = [
        pltpu.make_async_copy(field_ref.at[:, cam // 4, cam % 4], field.at[cam], arrived.at[cam])
        for cam in range(8)
    ]
    for copy in copies:
        copy.start()
    for cam in range(8):
        copies[cam].wait()
        for chunk in range(chunks):
            lanes = slice(chunk * LANES, (chunk + 1) * LANES)
            total = field[cam, 0, :, lanes].astype(F32) * weights_ref[0]
            for channel in range(1, 4):
                total = total + field[cam, channel, :, lanes].astype(F32) * weights_ref[channel]
            out_ref[chunk, cam * 16 : (cam + 1) * 16, :] = total.astype(BF16)
    row, lane = iota((16, LANES), 0), iota((16, LANES), 1)
    wanted = jnp.where(row < 3, row + 125, jnp.where(row == 3, 0, jnp.where(row == 4, 127, row - 5)))
    select = jnp.where((row < 8) & (lane == wanted), F32(1.0), F32(0.0)).astype(BF16)
    edges = [
        lax.dot_general(select, out_ref[chunk, 0:128, :], NT, preferred_element_type=F32)
        for chunk in range(chunks)
    ]
    zero = jnp.zeros((16, LANES), F32)
    for chunk in range(chunks):
        left = edges[chunk - 1] if chunk else zero
        right = edges[chunk + 1] if chunk < chunks - 1 else zero
        halo = jnp.where(row < 3, left, jnp.where(row < 5, edges[chunk], right))
        out_ref[chunk, 128:144, :] = halo.astype(BF16)


def turn_kernel(in_ref, out_ref, scratch):
    for c in range(8):
        for i in range(2):
            s = c * 2 + i
            block = in_ref[c, :, i * 64 : (i + 1) * 64, :].reshape(256, LANES)
            scratch[s] = block.astype(F32)
            for r in range(16):
                out_ref[r, s] = scratch[s, pl.ds(r, 16, stride=16), :].astype(BF16)


class Smoother:
    def __init__(self):
        self.last = [None] * 4

    def push(self, value):
        for n in range(4):
            before, self.last[n] = self.last[n], value
            if before is not None:
                value = before if value is None else value + before
        return value


def tensor_of_cameras(field, grad_img):
    count = len(field)
    smoothers = [Smoother() for _ in range(3)]
    result = [[] for _ in range(3)]
    for t in range(count + 2):
        products = (None,) * 3
        if t < count:
            if t == 0:
                grad_cam = -field[1]
            elif t == count - 1:
                grad_cam = field[t - 1]
            else:
                grad_cam = field[t - 1] - field[t + 1]
            products = (grad_cam * grad_cam, grad_cam * grad_img[t], grad_img[t] * grad_img[t])
        for f in range(3):
            value = smoothers[f].push(products[f])
            if t >= 2:
                result[f].append(value.astype(BF16))
    return result


def split(values):
    return [values[n * 16 : (n + 1) * 16] for n in range(values.shape[0] // 16)]


def horizontal_kernel(place_ref, in_ref, out_ref, edge, edge_sums, grads, smooths):
    k, u = iota((LANES, LANES), 0), iota((LANES, LANES), 1)
    d = k - u
    dist = jnp.abs(d)
    eye = ones_where((d == 0, 1.0)).astype(BF16)
    for col in range(4):
        rows = in_ref[:, col, 128:144, :].reshape(128, LANES)
        moved = lax.dot_general(eye, rows, NT, preferred_element_type=F32).astype(BF16)
        for i in range(2):
            edge[i, col * 64 : (col + 1) * 64, :] = moved[i * 64 : (i + 1) * 64]
    slot = u & 15
    used = ((k >> 4) == (u >> 4)) & ((slot == 1) | (slot == 2) | (slot == 5) | (slot == 6))
    grad = ones_where((used & (d == 1), 1.0), (used & (d == -1), -1.0)).astype(BF16)
    for i in range(2):
        values = edge[i]
        grad_img = jnp.dot(values, grad, preferred_element_type=F32)
        summed = tensor_of_cameras(split(values.astype(F32)), split(grad_img))
        for f in range(3):
            for t in range(16):
                edge_sums[f, i, t * 16 : (t + 1) * 16, :] = summed[f][t]

    place, last = place_ref[0], place_ref[1] - 1
    unit = 1.0 / 1024.0
    has_left = jnp.where(place > 0, F32(unit), F32(0.0))
    has_right = jnp.where(place < last, F32(unit), F32(0.0))
    h, col = iota((16, LANES), 0), iota((16, LANES), 1)
    grad_edge = ones_where(((h == 2) & (col == 0), -1.0), ((h == 5) & (col == 127), 1.0))
    left = ones_where(
        ((h == 1) & (col == 0), 1.0), ((h == 2) & (col == 0), 4.0), ((h == 2) & (col == 1), 1.0)
    )
    right = ones_where(
        ((h == 5) & (col == 127), 4.0),
        ((h == 5) & (col == 126), 1.0),
        ((h == 6) & (col == 127), 1.0),
    )
    smooth_edge = (left * has_left + right * has_right).astype(BF16)
    grad_edge = grad_edge.astype(BF16)
    grad_own = ones_where((d == 1, 1.0), (d == -1, -1.0)).astype(BF16)
    smooth_own = ones_where(
        (dist == 0, 6.0 * unit), (dist == 1, 4.0 * unit), (dist == 2, unit)
    ).astype(BF16)
    zero = jnp.zeros((16, LANES), BF16)
    for c in range(8):
        for matrix, own, side in ((grads, grad_own, grad_edge), (smooths, smooth_own, smooth_edge)):
            matrix[c, 0:128, :] = own
            for n in range(8):
                matrix[c, 128 + n * 16 : 144 + n * 16, :] = side if n == c else zero

    @pl.loop(0, 8)
    def _(c):
        for i in range(2):
            values = in_ref[c, :, i * 64 : (i + 1) * 64, :].reshape(256, LANES)
            grad_img = jnp.dot(
                jnp.concatenate([values, edge[i]], axis=1), grads[c], preferred_element_type=F32
            )
            summed = tensor_of_cameras(split(values.astype(F32)), split(grad_img))
            for f in range(3):
                part = jnp.concatenate(summed[f])
                out_ref[f, c * 2 + i] = jnp.dot(
                    jnp.concatenate([part, edge_sums[f, i]], axis=1),
                    smooths[c],
                    preferred_element_type=F32,
                )


def parts_of(jaa, jab, jbb):
    spread, total = jaa - jbb, jaa + jbb
    twice = jab + jab
    return spread * spread + twice * twice, total * total + 0.1, jab, jbb + 0.1


def merge(horizontal, vertical):
    nh, dh, bh, ah = parts_of(*horizontal)
    nv, dv, bv, av = parts_of(*vertical)
    p, q = nh * dv, nv * dh
    top = p * (bh * av) + q * (bv * ah)
    return top / ((p + q + 0.1 * (dh * dv)) * (ah * av))


def vertical_kernel(place_ref, gray_ref, low_ref, high_ref, hor_ref, out_ref, field, sums, turned):
    scale = F32(1.0 / 32.0)
    zero = jnp.zeros((22, 16, LANES), F32)
    field[0] = zero
    field[17] = zero

    @pl.loop(0, 16)
    def _(r):
        for s in range(16):
            field[s + 1, r + 3] = gray_ref[r, s].astype(F32) * scale

    for r in range(3):
        for s in range(16):
            field[s + 1, r] = low_ref[r, s].astype(F32) * scale
            field[s + 1, r + 19] = high_ref[r, s].astype(F32) * scale

    has_low = jnp.where(place_ref[0] > 0, F32(1.0), F32(0.0))
    has_high = jnp.where(place_ref[0] < place_ref[1] - 1, F32(1.0), F32(0.0))

    @pl.loop(0, 16)
    def _(s):
        smoothers = [Smoother() for _ in range(3)]
        for q in range(20):
            grad_cam = field[s, q + 1] - field[s + 2, q + 1]
            grad_img = field[s + 1, q + 2] - field[s + 1, q]
            if q < 2:
                grad_img = grad_img * has_low
            if q >= 18:
                grad_img = grad_img * has_high
            products = (grad_cam * grad_cam, grad_cam * grad_img, grad_img * grad_img)
            for f in range(3):
                value = smoothers[f].push(products[f])
                if q >= 4:
                    sums[f, s, q - 4] = value

    @pl.loop(0, 16)
    def _(r):
        smoothers = [Smoother() for _ in range(3)]
        rows = pl.ds(r, 16, stride=16)
        for s in range(18):
            vertical = [
                smoothers[f].push(sums[f, s, r] if s < 16 else None) for f in range(3)
            ]
            if s >= 2:
                horizontal = [hor_ref[f, s - 2, rows, :] for f in range(3)]
                turned[s - 2, rows, :] = merge(horizontal, vertical)

    @pl.loop(0, 8)
    def _(c):
        for i in range(2):
            out_ref[c, :, i] = turned[c * 2 + i].astype(BF16).reshape(4, 64, LANES)


def spread_kernel(chunks, in_ref, out_ref, scratch, sent):
    copies = []
    for part in range(8):
        rows = slice(part * 16, (part + 1) * 16)
        for chunk in range(chunks):
            scratch[rows, chunk * LANES : (chunk + 1) * LANES] = in_ref[chunk, rows, :].astype(F32)
        copy = pltpu.make_async_copy(scratch.at[rows], out_ref.at[rows], sent.at[part])
        copy.start()
        copies.append(copy)
    for copy in copies:
        copy.wait()


def per_device(light_field, channel_weights):
    group = ("crow", "ccol")
    chunks = lax.axis_size(group)
    band, bands = lax.axis_index("band"), lax.axis_size("band")
    params = lambda mib: pltpu.CompilerParams(vmem_limit_bytes=mib * MIB)
    smem = pl.BlockSpec(memory_space=pltpu.SMEM)
    vmem = pl.BlockSpec(memory_space=pltpu.VMEM)
    hbm = pl.BlockSpec(memory_space=pl.ANY)

    packed = pl.pallas_call(
        functools.partial(gray_kernel, chunks),
        in_specs=[smem, hbm],
        out_specs=vmem,
        out_shape=jax.ShapeDtypeStruct((chunks, 144, LANES), BF16),
        scratch_shapes=[pltpu.VMEM((8, 4, 16, chunks * LANES), BF16), pltpu.SemaphoreType.DMA((8,))],
        compiler_params=params(58),
        name="gray",
    )(channel_weights, light_field)
    columns = lax.all_to_all(packed, group, 0, 0, tiled=True).reshape(8, 4, 144, LANES)

    turned = pl.pallas_call(
        turn_kernel,
        in_specs=[vmem],
        out_specs=vmem,
        out_shape=jax.ShapeDtypeStruct((16, 16, 16, LANES), BF16),
        scratch_shapes=[pltpu.VMEM((16, 256, LANES), F32)],
        compiler_params=params(16),
        name="turn",
    )(columns)
    low = lax.ppermute(turned[13:16], "band", [(n, n + 1) for n in range(bands - 1)])
    high = lax.ppermute(turned[0:3], "band", [(n + 1, n) for n in range(bands - 1)])

    hor = pl.pallas_call(
        horizontal_kernel,
        in_specs=[smem, vmem],
        out_specs=vmem,
        out_shape=jax.ShapeDtypeStruct((3, 16, 256, LANES), F32),
        scratch_shapes=[
            pltpu.VMEM((2, 256, LANES), BF16),
            pltpu.VMEM((3, 2, 256, LANES), BF16),
            pltpu.VMEM((8, 256, LANES), BF16),
            pltpu.VMEM((8, 256, LANES), BF16),
        ],
        compiler_params=params(24),
        cost_estimate=pl.CostEstimate(flops=10**9, bytes_accessed=8 * MIB, transcendentals=0),
        name="horizontal",
    )(jnp.stack([lax.axis_index(group), chunks]).astype(jnp.int32), columns)

    depth = pl.pallas_call(
        vertical_kernel,
        in_specs=[smem, vmem, vmem, vmem, vmem],
        out_specs=vmem,
        out_shape=jax.ShapeDtypeStruct((8, 4, 2, 64, LANES), BF16),
        scratch_shapes=[
            pltpu.VMEM((18, 22, 16, LANES), F32),
            pltpu.VMEM((3, 16, 16, 16, LANES), F32),
            pltpu.VMEM((16, 256, LANES), F32),
        ],
        compiler_params=params(32),
        name="vertical",
    )(jnp.stack([band, bands]).astype(jnp.int32), turned, low, high, hor)

    back = lax.all_to_all(depth.reshape(chunks, 128, LANES), group, 0, 0, tiled=True)
    out = pl.pallas_call(
        functools.partial(spread_kernel, chunks),
        in_specs=[vmem],
        out_specs=hbm,
        out_shape=jax.ShapeDtypeStruct((128, chunks * LANES), F32),
        scratch_shapes=[pltpu.VMEM((128, chunks * LANES), F32), pltpu.SemaphoreType.DMA((8,))],
        compiler_params=params(58),
        name="spread",
    )(back)
    return out.reshape(2, 4, 16, chunks * LANES)


def solution(mesh):
    placed = (P(None, "crow", "ccol", "band", None), P())
    return jax.shard_map(
        per_device,
        mesh=mesh,
        in_specs=placed,
        out_specs=P("crow", "ccol", "band", None),
        check_vma=False,
    )
```

profile of v0, /device:TPU:9, one launch (start us, length us, event | category | flops | bytes accessed | tf_op | source)
XLA Modules:
  0.0 74.5 jit_solution(658928650573544395)
XLA Ops:
  0.0 4.6 %gray.1 = bf16[32,144,128]{2,1,0:T(8,128)(2,1)} custom-call(f32[4]{0:T(128)} %weights_ref.1, bf16[4,2,4,16,4096]{4,3,2,1,0:T(8,128)(2,1)} %field_ref.1), custom_call_target="tpu_custom_call" | custom-call | tf_op jit(solution)/shard_map/gray/pallas_call | solution.py:259
  4.6 8.6 %all-to-all-start = ((bf16[32,144,128]{2,1,0:T(8,128)(2,1)}), bf16[32,144,128]{2,1,0:T(8,128)(2,1)S(1)}, u32[]{:S(2)}, u32[]{:S(2)}) async-start(bf16[32,144,128]{2,1,0:T(8,128)(2,1)} %gray.1), calls=%async_computation | async-start | bytes 2359296 | tf_op jit(solution)/shard_map/all_to_all | solution.py:268
  13.2 0.1 pad_add_fusion.1.place_ref
  13.3 18.3 %all-to-all-done = bf16[32,144,128]{2,1,0:T(8,128)(2,1)S(1)} async-done(((bf16[32,144,128]{2,1,0:T(8,128)(2,1)}), bf16[32,144,128]{2,1,0:T(8,128)(2,1)S(1)}, u32[]{:S(2)}, u32[]{:S(2)}) %all-to-all-start) | async-done | bytes 1179680 | tf_op jit(solution)/shard_map/all_to_all | solution.py:268
  31.5 0.7 turn.1.gray_ref
  32.3 3.2 %collective-permute-start = (bf16[3,16,16,128]{3,2,1,0:T(8,128)(2,1)S(1)}, bf16[3,16,16,128]{3,2,1,0:T(8,128)(2,1)S(1)}, u32[]{:S(2)}, u32[]{:S(2)}) collective-permute-start(bf16[3,16,16,128]{3,2,1,0:T(8,128)(2,1)S(1)} %get-tuple-element.6), channel_id=1, source_target_pairs={{0,1},{1,2},{2,3},{4,5},{5,6},{6,7},{8,9},{9,10},{10,11},{12,13},{... | collective-permute-start | bytes 589832 | tf_op jit(solution)/shard_map/ppermute | solution.py:279
  35.5 2.1 %collective-permute-start.1 = (bf16[3,16,16,128]{3,2,1,0:T(8,128)(2,1)S(1)}, bf16[3,16,16,128]{3,2,1,0:T(8,128)(2,1)S(1)}, u32[]{:S(2)}, u32[]{:S(2)}) collective-permute-start(bf16[3,16,16,128]{3,2,1,0:T(8,128)(2,1)S(1)} %get-tuple-element.5), channel_id=1, source_target_pairs={{1,0},{2,1},{3,2},{5,4},{6,5},{7,6},{9,8},{10,9},{11,10},{13,12},{... | collective-permute-start | bytes 589832 | tf_op jit(solution)/shard_map/ppermute | solution.py:280
  37.6 0.1 pad_add_fusion.place_ref
  37.7 5.8 %horizontal.1.hor_ref = f32[3,16,256,128]{3,2,1,0:T(8,128)S(1)} custom-call(s32[2]{0:T(128)S(1)} %pad_add_fusion.1.place_ref, bf16[8,4,144,128]{3,2,1,0:T(8,128)(2,1)S(1)} %bitcast.6), custom_call_target="tpu_custom_call" | custom-call | flops 1000000000 | bytes 8388608 | tf_op jit(solution)/shard_map/horizontal/pallas_call | solution.py:282
  43.4 0.0 collective-permute-done.low_ref
  43.5 0.0 collective-permute-done.1.high_ref
  43.5 6.8 %vertical.1 = bf16[8,4,2,64,128]{4,3,2,1,0:T(8,128)(2,1)S(1)} custom-call(s32[2]{0:T(128)S(1)} %pad_add_fusion.place_ref, bf16[16,16,16,128]{3,2,1,0:T(8,128)(2,1)S(1)} %turn.1.gray_ref, bf16[3,16,16,128]{3,2,1,0:T(8,128)(2,1)S(1)} %collective-permute-done.low_ref, bf16[3,16,16,128]{3,2,1,0:T(8,128)(2,1)S(1)} %collective-permute-done.1.high_ref, ...), custom_call_target="tpu_custom_call" | custom-call | tf_op jit(solution)/shard_map/vertical/pallas_call | solution.py:298
  50.3 21.6 %all_to_all.10.in_ref = bf16[32,128,128]{2,1,0:T(8,128)(2,1)} all-to-all(bf16[32,128,128]{2,1,0:T(8,128)(2,1)S(1)} %bitcast.7), channel_id=1, replica_groups=mesh['crow'=8,'ccol'=4,'band'=4] {'crow','ccol'}, dimensions={0} | all-to-all | bytes 2097152 | tf_op jit(solution)/shard_map/all_to_all | solution.py:312
  71.9 2.6 %spread.1 = f32[128,4096]{1,0:T(8,128)} custom-call(bf16[32,128,128]{2,1,0:T(8,128)(2,1)} %all_to_all.10.in_ref), custom_call_target="tpu_custom_call" | custom-call | tf_op jit(solution)/shard_map/spread/pallas_call | solution.py:313
  (1 shorter events, 0.0 us)
Async XLA Ops:
  4.6 27.0 %all-to-all-start = ((bf16[32,144,128]{2,1,0:T(8,128)(2,1)}), bf16[32,144,128]{2,1,0:T(8,128)(2,1)S(1)}, u32[]{:S(2)}, u32[]{:S(2)}) async-start(bf16[32,144,128]{2,1,0:T(8,128)(2,1)} %gray.1), calls=%async_computation | async-start | bytes 2359296 | tf_op jit(solution)/shard_map/all_to_all | solution.py:268
  32.3 11.2 %collective-permute-start = (bf16[3,16,16,128]{3,2,1,0:T(8,128)(2,1)S(1)}, bf16[3,16,16,128]{3,2,1,0:T(8,128)(2,1)S(1)}, u32[]{:S(2)}, u32[]{:S(2)}) collective-permute-start(bf16[3,16,16,128]{3,2,1,0:T(8,128)(2,1)S(1)} %get-tuple-element.6), channel_id=1, source_target_pairs={{0,1},{1,2},{2,3},{4,5},{5,6},{6,7},{8,9},{9,10},{10,11},{12,13},{... | collective-permute-start | bytes 589832 | tf_op jit(solution)/shard_map/ppermute | solution.py:279
  35.5 8.0 %collective-permute-start.1 = (bf16[3,16,16,128]{3,2,1,0:T(8,128)(2,1)S(1)}, bf16[3,16,16,128]{3,2,1,0:T(8,128)(2,1)S(1)}, u32[]{:S(2)}, u32[]{:S(2)}) collective-permute-start(bf16[3,16,16,128]{3,2,1,0:T(8,128)(2,1)S(1)} %get-tuple-element.5), channel_id=1, source_target_pairs={{1,0},{2,1},{3,2},{5,4},{6,5},{7,6},{9,8},{10,9},{11,10},{13,12},{... | collective-permute-start | bytes 589832 | tf_op jit(solution)/shard_map/ppermute | solution.py:280
where the time goes:
time: 75.7 us; the launch traced here: 74.5 us
  blocking collectives  21.6 us (29%)
  Pallas kernels  20.5 us (27%)
  waiting for transfers between devices  18.3 us (24%)
  starting transfers between devices  13.9 us (18%)
    all_to_all x1, blocking collectives, per_device(): lax.all_to_all(depth.reshape(chunks, 128, LANES), group, 0, 0, tiled=True)  21.6 us
    all_to_all x1, waiting for transfers between devices, per_device(): lax.all_to_all(packed, group, 0, 0, tiled=True).reshape(8, 4, 144, LANES)  18.3 us
    all_to_all x1, starting transfers between devices, per_device(): lax.all_to_all(packed, group, 0, 0, tiled=True).reshape(8, 4, 144, LANES)  8.61 us
    pallas_call x1, Pallas kernels, per_device(): pl.pallas_call(vertical_kernel, in_specs=[smem, vmem, vmem, vmem, vmem],...  6.84 us
    pallas_call x1, Pallas kernels, per_device(): pl.pallas_call(horizontal_kernel, in_specs=[smem, vmem], out_specs=vmem,...  5.76 us
    pallas_call x1, Pallas kernels, per_device(): pl.pallas_call(functools.partial(gray_kernel, chunks), in_specs=[smem, hb...  4.55 us
    ppermute x1, starting transfers between devices, per_device(): lax.ppermute(turned[13:16], 'band', [(n, n + 1) for n in range(bands - 1)])  3.2 us
    pallas_call x1, Pallas kernels, per_device(): pl.pallas_call(functools.partial(spread_kernel, chunks), in_specs=[vmem],...  2.62 us
  transfers between devices with their start and end apart: 3, of which 1 were waited for; matrix products, arithmetic and copies ran while one was open for 0% of the time, Pallas kernels for 8%

commit v1 on v0

v1 whole, which is shorter than its diff:
```python
import functools

import jax
import jax.numpy as jnp
from jax import lax
from jax.experimental import pallas as pl
from jax.experimental.pallas import tpu as pltpu
from jax.sharding import PartitionSpec as P

F32, BF16 = jnp.float32, jnp.bfloat16
LANES = 128
MIB = 1 << 20
NT = (((1,), (1,)), ((), ()))


def iota(shape, dim):
    return lax.broadcasted_iota(jnp.int32, shape, dim)


def ones_where(*conditions_and_values):
    total = None
    for condition, value in conditions_and_values:
        term = jnp.where(condition, F32(value), F32(0.0))
        total = term if total is None else total + term
    return total


def gray_kernel(chunks, weights_hbm, field_ref, out_ref, field, edges, weights_ref, arrived, known):
    def incoming(cam):
        return pltpu.make_async_copy(
            field_ref.at[:, cam // 4, cam % 4], field.at[cam], arrived.at[cam]
        )

    weights_copy = pltpu.make_async_copy(weights_hbm, weights_ref, known)
    weights_copy.start()
    for cam in range(8):
        incoming(cam).start()
    row, lane = iota((16, LANES), 0), iota((16, LANES), 1)
    wanted = jnp.where(row < 3, row + 125, jnp.where(row == 3, 0, jnp.where(row == 4, 127, row - 5)))
    select = jnp.where((row < 8) & (lane == wanted), F32(1.0), F32(0.0)).astype(BF16)
    edges[0] = jnp.zeros((16, LANES), F32)
    edges[chunks + 1] = jnp.zeros((16, LANES), F32)
    weights_copy.wait()
    weights = [weights_ref[channel] for channel in range(4)]

    @pl.loop(0, 8)
    def _(cam):
        incoming(cam).wait()
        rows = pl.ds(pl.multiple_of(cam * 16, 16), 16)
        for chunk in range(chunks):
            lanes = slice(chunk * LANES, (chunk + 1) * LANES)
            total = field[cam, 0, :, lanes].astype(F32) * weights[0]
            for channel in range(1, 4):
                total = total + field[cam, channel, :, lanes].astype(F32) * weights[channel]
            out_ref[chunk, rows, :] = total.astype(BF16)

    @pl.loop(0, chunks, unroll=32)
    def _(chunk):
        edges[chunk + 1] = lax.dot_general(
            select, out_ref[chunk, 0:128, :], NT, preferred_element_type=F32
        )

    @pl.loop(0, chunks, unroll=32)
    def _(chunk):
        halo = jnp.where(row < 3, edges[chunk], jnp.where(row < 5, edges[chunk + 1], edges[chunk + 2]))
        out_ref[chunk, 128:144, :] = halo.astype(BF16)


PITCH = 17


def edges_kernel(in_ref, first_ref, last_ref, scratch):
    for c in range(8):
        for i in range(2):
            s = c * 2 + i
            for t in range(16):
                rows = slice(i * 64 + t % 4 * 16, i * 64 + t % 4 * 16 + 16)
                scratch[s, t * PITCH : t * PITCH + 16, :] = in_ref[c, t // 4, rows, :].astype(F32)
            for r in range(3):
                first_ref[r, s] = scratch[s, pl.ds(r, 16, stride=PITCH), :].astype(BF16)
                last_ref[r, s] = scratch[s, pl.ds(r + 13, 16, stride=PITCH), :].astype(BF16)


class Smoother:
    def __init__(self):
        self.last = [None] * 4

    def push(self, value):
        for n in range(4):
            before, self.last[n] = self.last[n], value
            if before is not None:
                value = before if value is None else value + before
        return value


def tensor_of_cameras(field, grad_img):
    count = len(field)
    smoothers = [Smoother() for _ in range(3)]
    result = [[] for _ in range(3)]
    for t in range(count + 2):
        products = (None,) * 3
        if t < count:
            if t == 0:
                grad_cam = -field[1]
            elif t == count - 1:
                grad_cam = field[t - 1]
            else:
                grad_cam = field[t - 1] - field[t + 1]
            products = (grad_cam * grad_cam, grad_cam * grad_img[t], grad_img[t] * grad_img[t])
        for f in range(3):
            value = smoothers[f].push(products[f])
            if t >= 2:
                result[f].append(value.astype(BF16))
    return result


def split(values):
    return [values[n * 16 : (n + 1) * 16] for n in range(values.shape[0] // 16)]


def horizontal_kernel(in_ref, out_ref, gray_ref, edge, edge_sums, grads, smooths, scratch):
    k, u = iota((LANES, LANES), 0), iota((LANES, LANES), 1)
    d = k - u
    dist = jnp.abs(d)
    eye = ones_where((d == 0, 1.0)).astype(BF16)
    for col in range(4):
        rows = in_ref[:, col, 128:144, :].reshape(128, LANES)
        moved = lax.dot_general(eye, rows, NT, preferred_element_type=F32).astype(BF16)
        for i in range(2):
            edge[i, col * 64 : (col + 1) * 64, :] = moved[i * 64 : (i + 1) * 64]
    slot = u & 15
    used = ((k >> 4) == (u >> 4)) & ((slot == 1) | (slot == 2) | (slot == 5) | (slot == 6))
    grad = ones_where((used & (d == 1), 1.0), (used & (d == -1), -1.0)).astype(BF16)
    for i in range(2):
        values = edge[i]
        grad_img = jnp.dot(values, grad, preferred_element_type=F32)
        summed = tensor_of_cameras(split(values.astype(F32)), split(grad_img))
        for f in range(3):
            for t in range(16):
                edge_sums[f, i, t * 16 : (t + 1) * 16, :] = summed[f][t]

    group = ("crow", "ccol")
    place, last = lax.axis_index(group), lax.axis_size(group) - 1
    unit = 1.0 / 1024.0
    has_left = jnp.where(place > 0, F32(unit), F32(0.0))
    has_right = jnp.where(place < last, F32(unit), F32(0.0))
    h, col = iota((16, LANES), 0), iota((16, LANES), 1)
    grad_edge = ones_where(((h == 2) & (col == 0), -1.0), ((h == 5) & (col == 127), 1.0))
    left = ones_where(
        ((h == 1) & (col == 0), 1.0), ((h == 2) & (col == 0), 4.0), ((h == 2) & (col == 1), 1.0)
    )
    right = ones_where(
        ((h == 5) & (col == 127), 4.0),
        ((h == 5) & (col == 126), 1.0),
        ((h == 6) & (col == 127), 1.0),
    )
    smooth_edge = (left * has_left + right * has_right).astype(BF16)
    grad_edge = grad_edge.astype(BF16)
    grad_own = ones_where((d == 1, 1.0), (d == -1, -1.0)).astype(BF16)
    smooth_own = ones_where(
        (dist == 0, 6.0 * unit), (dist == 1, 4.0 * unit), (dist == 2, unit)
    ).astype(BF16)
    zero = jnp.zeros((16, LANES), BF16)
    for c in range(8):
        for matrix, own, side in ((grads, grad_own, grad_edge), (smooths, smooth_own, smooth_edge)):
            matrix[c, 0:128, :] = own
            for n in range(8):
                matrix[c, 128 + n * 16 : 144 + n * 16, :] = side if n == c else zero

    def values_of(c, i):
        return in_ref[c, :, i * 64 : (i + 1) * 64, :].reshape(256, LANES)

    def gradient(c):
        own = jnp.concatenate([values_of(c, 0), values_of(c, 1)])
        side = jnp.concatenate([edge[0], edge[1]])
        return jnp.dot(
            jnp.concatenate([own, side], axis=1), grads[c], preferred_element_type=F32
        )

    def products(c, grad_img):
        summed = []
        for i in range(2):
            field = split(values_of(c, i).astype(F32))
            for t in range(16):
                scratch[c * 2 + i, t * PITCH : t * PITCH + 16, :] = field[t]
            for r in range(16):
                gray_ref[c * 2 + i, r] = scratch[c * 2 + i, pl.ds(r, 16, stride=PITCH), :]
            summed.append(tensor_of_cameras(field, split(grad_img[i * 256 : (i + 1) * 256])))
        return jnp.concatenate([v for f in range(3) for i in range(2) for v in summed[i][f]])

    def smooth(c, parts):
        side = jnp.concatenate([edge_sums[f, i] for f in range(3) for i in range(2)])
        full = jnp.dot(
            jnp.concatenate([parts, side], axis=1), smooths[c], preferred_element_type=F32
        )
        for f in range(3):
            for i in range(2):
                n = (f * 2 + i) * 256
                out_ref[f, c * 2 + i] = full[n : n + 256]

    grad_img, parts = gradient(0), None
    for c in range(8):
        following = gradient(c + 1) if c < 7 else None
        now = products(c, grad_img)
        if c:
            smooth(c - 1, parts)
        grad_img, parts = following, now
    smooth(7, parts)


def parts_of(jaa, jab, jbb, scale):
    spread, total = jaa - jbb, jaa + jbb
    twice = jab + jab
    near = F32(0.1 * scale)
    return spread * spread + twice * twice, total * total + near * F32(scale), jab, jbb + near


def merge(horizontal, vertical):
    nh, dh, bh, ah = parts_of(*horizontal, 1.0)
    nv, dv, bv, av = parts_of(*vertical, 1024.0)
    p, q = nh * dv, nv * dh
    top = p * (bh * av) + q * (bv * ah)
    return top / ((p + q + 0.1 * (dh * dv)) * (ah * av))


def vertical_kernel(gray_ref, low_ref, high_ref, hor_ref, out_ref, sums):
    band, last = lax.axis_index("band"), lax.axis_size("band") - 1
    has_low = jnp.where(band > 0, F32(1.0), F32(0.0))
    has_high = jnp.where(band < last, F32(1.0), F32(0.0))

    def field(s, r):
        if r < 0:
            return low_ref[r + 3, s].astype(F32)
        return gray_ref[s, r] if r < 16 else high_ref[r - 16, s].astype(F32)

    for s in range(16):
        smoothers = [Smoother() for _ in range(3)]
        for q in range(20):
            r = q - 2
            if s == 0:
                grad_cam = -field(1, r)
            elif s == 15:
                grad_cam = field(14, r)
            else:
                grad_cam = field(s - 1, r) - field(s + 1, r)
            grad_img = field(s, r + 1) - field(s, r - 1)
            if r < 0:
                grad_img = grad_img * has_low
            if r >= 16:
                grad_img = grad_img * has_high
            products = (grad_cam * grad_cam, grad_cam * grad_img, grad_img * grad_img)
            for f in range(3):
                value = smoothers[f].push(products[f])
                if q >= 4:
                    sums[f, s, pl.ds(q - 4, 16, stride=PITCH), :] = value

    for t in range(16):
        smoothers = [Smoother() for _ in range(3)]
        for s in range(18):
            vertical = [
                smoothers[f].push(sums[f, s, t * PITCH : t * PITCH + 16, :] if s < 16 else None)
                for f in range(3)
            ]
            if s >= 2:
                c, i = (s - 2) // 2, (s - 2) % 2
                horizontal = [hor_ref[f, s - 2, t * 16 : (t + 1) * 16, :] for f in range(3)]
                rows = slice(t % 4 * 16, t % 4 * 16 + 16)
                out_ref[c, t // 4, i, rows, :] = merge(horizontal, vertical).astype(BF16)


def spread_kernel(chunks, in_ref, out_ref, scratch, sent):
    copies = []
    for part in range(8):
        rows = slice(part * 16, (part + 1) * 16)
        for chunk in range(chunks):
            scratch[rows, chunk * LANES : (chunk + 1) * LANES] = in_ref[chunk, rows, :].astype(F32)
        copy = pltpu.make_async_copy(scratch.at[rows], out_ref.at[rows], sent.at[part])
        copy.start()
        copies.append(copy)
    for copy in copies:
        copy.wait()


def per_device(light_field, channel_weights):
    group = ("crow", "ccol")
    chunks = lax.axis_size(group)
    bands = lax.axis_size("band")
    params = lambda mib: pltpu.CompilerParams(vmem_limit_bytes=mib * MIB)
    vmem = pl.BlockSpec(memory_space=pltpu.VMEM)
    hbm = pl.BlockSpec(memory_space=pl.ANY)

    packed = pl.pallas_call(
        functools.partial(gray_kernel, chunks),
        in_specs=[hbm, hbm],
        out_specs=vmem,
        out_shape=jax.ShapeDtypeStruct((chunks, 144, LANES), BF16),
        scratch_shapes=[
            pltpu.VMEM((8, 4, 16, chunks * LANES), BF16),
            pltpu.VMEM((chunks + 2, 16, LANES), F32),
            pltpu.SMEM((4,), F32),
            pltpu.SemaphoreType.DMA((8,)),
            pltpu.SemaphoreType.DMA,
        ],
        compiler_params=params(58),
        name="gray",
    )(channel_weights, light_field)
    columns = lax.all_to_all(packed, group, 0, 0, tiled=True).reshape(8, 4, 144, LANES)

    first, final = pl.pallas_call(
        edges_kernel,
        in_specs=[vmem],
        out_specs=[vmem, vmem],
        out_shape=[jax.ShapeDtypeStruct((3, 16, 16, LANES), BF16)] * 2,
        scratch_shapes=[pltpu.VMEM((16, 16 * PITCH, LANES), F32)],
        compiler_params=params(16),
        name="edges",
    )(columns)
    low = lax.ppermute(final, "band", [(n, n + 1) for n in range(bands - 1)])
    high = lax.ppermute(first, "band", [(n + 1, n) for n in range(bands - 1)])

    hor, gray = pl.pallas_call(
        horizontal_kernel,
        in_specs=[vmem],
        out_specs=[vmem, vmem],
        out_shape=[
            jax.ShapeDtypeStruct((3, 16, 256, LANES), F32),
            jax.ShapeDtypeStruct((16, 16, 16, LANES), F32),
        ],
        scratch_shapes=[
            pltpu.VMEM((2, 256, LANES), BF16),
            pltpu.VMEM((3, 2, 256, LANES), BF16),
            pltpu.VMEM((8, 256, LANES), BF16),
            pltpu.VMEM((8, 256, LANES), BF16),
            pltpu.VMEM((16, 16 * PITCH, LANES), F32),
        ],
        compiler_params=params(24),
        cost_estimate=pl.CostEstimate(flops=10**9, bytes_accessed=8 * MIB, transcendentals=0),
        name="horizontal",
    )(columns)

    depth = pl.pallas_call(
        vertical_kernel,
        in_specs=[vmem, vmem, vmem, vmem],
        out_specs=vmem,
        out_shape=jax.ShapeDtypeStruct((8, 4, 2, 64, LANES), BF16),
        scratch_shapes=[pltpu.VMEM((3, 16, 16 * PITCH, LANES), F32)],
        compiler_params=params(24),
        name="vertical",
    )(gray, low, high, hor)

    back = lax.all_to_all(depth.reshape(chunks, 128, LANES), group, 0, 0, tiled=True)
    out = pl.pallas_call(
        functools.partial(spread_kernel, chunks),
        in_specs=[vmem],
        out_specs=hbm,
        out_shape=jax.ShapeDtypeStruct((128, chunks * LANES), F32),
        scratch_shapes=[pltpu.VMEM((128, chunks * LANES), F32), pltpu.SemaphoreType.DMA((8,))],
        compiler_params=params(8),
        name="spread",
    )(back)
    return out.reshape(2, 4, 16, chunks * LANES)


def solution(mesh):
    placed = (P(None, "crow", "ccol", "band", None), P())
    return jax.shard_map(
        per_device,
        mesh=mesh,
        in_specs=placed,
        out_specs=P("crow", "ccol", "band", None),
        check_vma=False,
    )
```

time: 75.7 us -> 71.2 us (0.941)
  blocking collectives: 21.6 us -> 49 us
  waiting for transfers between devices: 18.3 us -> 2.27 us
  starting transfers between devices: 13.9 us -> 5.29 us
  Pallas kernels: 20.5 us -> 13.4 us
    all_to_all x0 -> x1, blocking collectives: none -> 27.6 us  [per_device(): lax.all_to_all(packed, group, 0, 0, tiled=True).reshape(8, 4, 144, LANES)]
    all_to_all x1 -> x0, waiting for transfers between devices: 18.3 us -> none  [per_device(): lax.all_to_all(packed, group, 0, 0, tiled=True).reshape(8, 4, 144, LANES)]
    all_to_all x1 -> x0, starting transfers between devices: 8.61 us -> none  [per_device(): lax.all_to_all(packed, group, 0, 0, tiled=True).reshape(8, 4, 144, LANES)]
    pallas_call x4, Pallas kernels: 17.9 us -> 12 us  [the longest x1 4.5 us: per_device(): pl.pallas_call(vertical_kernel, in_specs=[vmem, vmem, vmem, vmem], out_sp...]
    ppermute x2, waiting for transfers between devices: 0.01 us -> 2.27 us  [the longest x1 2.27 us: per_device(): high = lax.ppermute(first, 'band', [(n + 1, n) for n in range(bands - 1)])]
    pallas_call x1, Pallas kernels: 2.62 us -> 1.39 us  [per_device(): pl.pallas_call(functools.partial(spread_kernel, chunks), in_specs=[vmem],...]
  transfers between devices with their start and end apart: 3 -> 2, of which waited for: 1 -> 1; matrix products, arithmetic and copies ran while one was open for 0% -> 0% of each run, Pallas kernels for 8% -> 5%
where the time goes in v1:
time: 71.2 us; the launch traced here: 70.1 us
  blocking collectives  49 us (69%)
  Pallas kernels  13.4 us (19%)
  starting transfers between devices  5.29 us (7%)
  waiting for transfers between devices  2.27 us (3%)
    all_to_all x1, blocking collectives, per_device(): lax.all_to_all(packed, group, 0, 0, tiled=True).reshape(8, 4, 144, LANES)  27.6 us
    all_to_all x1, blocking collectives, per_device(): lax.all_to_all(depth.reshape(chunks, 128, LANES), group, 0, 0, tiled=True)  21.5 us
    pallas_call x1, Pallas kernels, per_device(): pl.pallas_call(vertical_kernel, in_specs=[vmem, vmem, vmem, vmem], out_sp...  4.5 us
    pallas_call x1, Pallas kernels, per_device(): pl.pallas_call(functools.partial(gray_kernel, chunks), in_specs=[hbm, hbm...  4 us
    pallas_call x1, Pallas kernels, per_device(): pl.pallas_call(horizontal_kernel, in_specs=[vmem], out_specs=[vmem, vmem]...  3.29 us
    ppermute x1, starting transfers between devices, per_device(): low = lax.ppermute(final, 'band', [(n, n + 1) for n in range(bands - 1)])  3.2 us
    ppermute x1, waiting for transfers between devices, per_device(): high = lax.ppermute(first, 'band', [(n + 1, n) for n in range(bands - 1)])  2.27 us
    ppermute x1, starting transfers between devices, per_device(): high = lax.ppermute(first, 'band', [(n + 1, n) for n in range(bands - 1)])  2.09 us
  transfers between devices with their start and end apart: 2, of which 1 were waited for; matrix products, arithmetic and copies ran while one was open for 0% of the time, Pallas kernels for 5%

profile of v1, /device:TPU:9, one launch (start us, length us, event | category | flops | bytes accessed | tf_op | source)
XLA Modules:
  0.0 70.1 jit_solution(7413575677503821965)
XLA Ops:
  0.0 4.0 %gray.1 = bf16[32,144,128]{2,1,0:T(8,128)(2,1)} custom-call(f32[4]{0:T(128)} %weights_hbm.1, bf16[4,2,4,16,4096]{4,3,2,1,0:T(8,128)(2,1)} %field_ref.1), custom_call_target="tpu_custom_call" | custom-call | tf_op jit(solution)/shard_map/gray/pallas_call | solution.py:292
  4.0 27.6 %all_to_all.10 = bf16[32,144,128]{2,1,0:T(8,128)(2,1)S(1)} all-to-all(bf16[32,144,128]{2,1,0:T(8,128)(2,1)} %gray.1), channel_id=1, replica_groups=mesh['crow'=8,'ccol'=4,'band'=4] {'crow','ccol'}, dimensions={0} | all-to-all | bytes 2359296 | tf_op jit(solution)/shard_map/all_to_all | solution.py:307
  31.6 0.2 edges.1
  31.8 3.2 %collective-permute-start = (bf16[3,16,16,128]{3,2,1,0:T(8,128)(2,1)S(1)}, bf16[3,16,16,128]{3,2,1,0:T(8,128)(2,1)S(1)}, u32[]{:S(2)}, u32[]{:S(2)}) collective-permute-start(bf16[3,16,16,128]{3,2,1,0:T(8,128)(2,1)S(1)} %get-tuple-element.10), channel_id=1, source_target_pairs={{0,1},{1,2},{2,3},{4,5},{5,6},{6,7},{8,9},{9,10},{10,11},{12,13},{... | collective-permute-start | bytes 589832 | tf_op jit(solution)/shard_map/ppermute | solution.py:318
  35.0 2.1 %collective-permute-start.1 = (bf16[3,16,16,128]{3,2,1,0:T(8,128)(2,1)S(1)}, bf16[3,16,16,128]{3,2,1,0:T(8,128)(2,1)S(1)}, u32[]{:S(2)}, u32[]{:S(2)}) collective-permute-start(bf16[3,16,16,128]{3,2,1,0:T(8,128)(2,1)S(1)} %get-tuple-element.11), channel_id=1, source_target_pairs={{1,0},{2,1},{3,2},{5,4},{6,5},{7,6},{9,8},{10,9},{11,10},{13,12},{... | collective-permute-start | bytes 589832 | tf_op jit(solution)/shard_map/ppermute | solution.py:319
  37.1 3.3 %horizontal.1 = (f32[3,16,256,128]{3,2,1,0:T(8,128)S(1)}, f32[16,16,16,128]{3,2,1,0:T(8,128)S(1)}) custom-call(bf16[8,4,144,128]{3,2,1,0:T(8,128)(2,1)S(1)} %bitcast.4), custom_call_target="tpu_custom_call" | custom-call | flops 1000000000 | bytes 8388608 | tf_op jit(solution)/shard_map/horizontal/pallas_call | solution.py:321
  40.4 0.0 collective-permute-done.low_ref
  40.4 2.3 %collective-permute-done.1.high_ref = bf16[3,16,16,128]{3,2,1,0:T(8,128)(2,1)S(1)} collective-permute-done((bf16[3,16,16,128]{3,2,1,0:T(8,128)(2,1)S(1)}, bf16[3,16,16,128]{3,2,1,0:T(8,128)(2,1)S(1)}, u32[]{:S(2)}, u32[]{:S(2)}) %collective-permute-start.1) | collective-permute-done | bytes 196640 | tf_op jit(solution)/shard_map/ppermute | solution.py:319
  42.7 4.5 %vertical.1 = bf16[8,4,2,64,128]{4,3,2,1,0:T(8,128)(2,1)S(1)} custom-call(f32[16,16,16,128]{3,2,1,0:T(8,128)S(1)} %get-tuple-element.9.gray_ref, bf16[3,16,16,128]{3,2,1,0:T(8,128)(2,1)S(1)} %collective-permute-done.low_ref, bf16[3,16,16,128]{3,2,1,0:T(8,128)(2,1)S(1)} %collective-permute-done.1.high_ref, f32[3,16,256,128]{3,2,1,0:T(8,128)S(1)} %get-tuple-element.12.hor_ref), custom_call_target="tpu_custom_call" | custom-call | tf_op jit(solution)/shard_map/vertical/pallas_call | solution.py:341
  47.2 21.5 %all_to_all.11.in_ref = bf16[32,128,128]{2,1,0:T(8,128)(2,1)S(1)} all-to-all(bf16[32,128,128]{2,1,0:T(8,128)(2,1)S(1)} %bitcast.5), channel_id=1, replica_groups=mesh['crow'=8,'ccol'=4,'band'=4] {'crow','ccol'}, dimensions={0} | all-to-all | bytes 2097152 | tf_op jit(solution)/shard_map/all_to_all | solution.py:351
  68.7 1.4 %spread.1 = f32[128,4096]{1,0:T(8,128)} custom-call(bf16[32,128,128]{2,1,0:T(8,128)(2,1)S(1)} %all_to_all.11.in_ref), custom_call_target="tpu_custom_call" | custom-call | tf_op jit(solution)/shard_map/spread/pallas_call | solution.py:352
Async XLA Ops:
  31.8 8.6 %collective-permute-start = (bf16[3,16,16,128]{3,2,1,0:T(8,128)(2,1)S(1)}, bf16[3,16,16,128]{3,2,1,0:T(8,128)(2,1)S(1)}, u32[]{:S(2)}, u32[]{:S(2)}) collective-permute-start(bf16[3,16,16,128]{3,2,1,0:T(8,128)(2,1)S(1)} %get-tuple-element.10), channel_id=1, source_target_pairs={{0,1},{1,2},{2,3},{4,5},{5,6},{6,7},{8,9},{9,10},{10,11},{12,13},{... | collective-permute-start | bytes 589832 | tf_op jit(solution)/shard_map/ppermute | solution.py:318
  35.0 7.7 %collective-permute-start.1 = (bf16[3,16,16,128]{3,2,1,0:T(8,128)(2,1)S(1)}, bf16[3,16,16,128]{3,2,1,0:T(8,128)(2,1)S(1)}, u32[]{:S(2)}, u32[]{:S(2)}) collective-permute-start(bf16[3,16,16,128]{3,2,1,0:T(8,128)(2,1)S(1)} %get-tuple-element.11), channel_id=1, source_target_pairs={{1,0},{2,1},{3,2},{5,4},{6,5},{7,6},{9,8},{10,9},{11,10},{13,12},{... | collective-permute-start | bytes 589832 | tf_op jit(solution)/shard_map/ppermute | solution.py:319

commit v2 on v1

--- a/solution.py
+++ b/solution.py
@@ -63,7 +63,7 @@
     @pl.loop(0, chunks, unroll=32)
     def _(chunk):
         halo = jnp.where(row < 3, edges[chunk], jnp.where(row < 5, edges[chunk + 1], edges[chunk + 2]))
-        out_ref[chunk, 128:144, :] = halo.astype(BF16)
+        out_ref[chunk, 128:136, :] = halo[0:8].astype(BF16)
 
 
 PITCH = 17
@@ -118,18 +118,45 @@
     return [values[n * 16 : (n + 1) * 16] for n in range(values.shape[0] // 16)]
 
 
-def horizontal_kernel(in_ref, out_ref, gray_ref, edge, edge_sums, grads, smooths, scratch):
+def products_of(field, s, r, factor=None):
+    if s == 0:
+        grad_cam = -field(1, r)
+    elif s == 15:
+        grad_cam = field(14, r)
+    else:
+        grad_cam = field(s - 1, r) - field(s + 1, r)
+    grad_img = field(s, r + 1) - field(s, r - 1)
+    if factor is not None:
+        grad_img = grad_img * factor
+    return grad_cam * grad_cam, grad_cam * grad_img, grad_img * grad_img
+
+
+def merge_rows(rows, sums, hor_ref, depth_ref):
+    for n, r in enumerate(rows):
+        smoothers = [Smoother() for _ in range(3)]
+        lines = pl.ds(r, 16, stride=PITCH)
+        for s in range(18):
+            vertical = [smoothers[f].push(sums[f, s, n] if s < 16 else None) for f in range(3)]
+            if s >= 2:
+                horizontal = [hor_ref[f, s - 2, lines, :] for f in range(3)]
+                depth_ref[s - 2, lines, :] = merge(horizontal, vertical)
+
+
+def inner_kernel(
+    in_ref, out_ref, gray_ref, depth_ref, edge, edge_sums, grads, smooths, scratch, sums
+):
     k, u = iota((LANES, LANES), 0), iota((LANES, LANES), 1)
     d = k - u
     dist = jnp.abs(d)
     eye = ones_where((d == 0, 1.0)).astype(BF16)
     for col in range(4):
-        rows = in_ref[:, col, 128:144, :].reshape(128, LANES)
+        rows = [in_ref[c, col, 128:136, :].astype(F32) for c in range(8)]
+        rows = jnp.concatenate(rows + [jnp.zeros((64, LANES), F32)]).astype(BF16)
         moved = lax.dot_general(eye, rows, NT, preferred_element_type=F32).astype(BF16)
         for i in range(2):
             edge[i, col * 64 : (col + 1) * 64, :] = moved[i * 64 : (i + 1) * 64]
-    slot = u & 15
-    used = ((k >> 4) == (u >> 4)) & ((slot == 1) | (slot == 2) | (slot == 5) | (slot == 6))
+    slot = u & 7
+    used = ((k >> 3) == (u >> 3)) & ((slot == 1) | (slot == 2) | (slot == 5) | (slot == 6))
     grad = ones_where((used & (d == 1), 1.0), (used & (d == -1), -1.0)).astype(BF16)
     for i in range(2):
         values = edge[i]
@@ -144,7 +171,7 @@
     unit = 1.0 / 1024.0
     has_left = jnp.where(place > 0, F32(unit), F32(0.0))
     has_right = jnp.where(place < last, F32(unit), F32(0.0))
-    h, col = iota((16, LANES), 0), iota((16, LANES), 1)
+    h, col = iota((8, LANES), 0), iota((8, LANES), 1)
     grad_edge = ones_where(((h == 2) & (col == 0), -1.0), ((h == 5) & (col == 127), 1.0))
     left = ones_where(
         ((h == 1) & (col == 0), 1.0), ((h == 2) & (col == 0), 4.0), ((h == 2) & (col == 1), 1.0)
@@ -154,18 +181,18 @@
         ((h == 5) & (col == 126), 1.0),
         ((h == 6) & (col == 127), 1.0),
     )
-    smooth_edge = (left * has_left + right * has_right).astype(BF16)
-    grad_edge = grad_edge.astype(BF16)
+    smooth_edge = left * has_left + right * has_right
     grad_own = ones_where((d == 1, 1.0), (d == -1, -1.0)).astype(BF16)
     smooth_own = ones_where(
         (dist == 0, 6.0 * unit), (dist == 1, 4.0 * unit), (dist == 2, unit)
     ).astype(BF16)
-    zero = jnp.zeros((16, LANES), BF16)
+    zero = jnp.zeros((8, LANES), F32)
     for c in range(8):
         for matrix, own, side in ((grads, grad_own, grad_edge), (smooths, smooth_own, smooth_edge)):
             matrix[c, 0:128, :] = own
             for n in range(8):
-                matrix[c, 128 + n * 16 : 144 + n * 16, :] = side if n == c else zero
+                pair = [side if n * 2 + m == c else zero for m in range(2)]
+                matrix[c, 128 + n * 16 : 144 + n * 16, :] = jnp.concatenate(pair).astype(BF16)
 
     def values_of(c, i):
         return in_ref[c, :, i * 64 : (i + 1) * 64, :].reshape(256, LANES)
@@ -196,7 +223,9 @@
         for f in range(3):
             for i in range(2):
                 n = (f * 2 + i) * 256
-                out_ref[f, c * 2 + i] = full[n : n + 256]
+                for t in range(16):
+                    rows = slice(t * PITCH, t * PITCH + 16)
+                    out_ref[f, c * 2 + i, rows, :] = full[n + t * 16 : n + t * 16 + 16]
 
     grad_img, parts = gradient(0), None
     for c in range(8):
@@ -207,6 +236,16 @@
         grad_img, parts = following, now
     smooth(7, parts)
 
+    for s in range(16):
+        smoothers = [Smoother() for _ in range(3)]
+        for r in range(1, 15):
+            products = products_of(lambda s, r: gray_ref[s, r], s, r)
+            for f in range(3):
+                value = smoothers[f].push(products[f])
+                if r >= 5:
+                    sums[f, s, r - 5] = value
+    merge_rows(range(3, 13), sums, out_ref, depth_ref)
+
 
 def parts_of(jaa, jab, jbb, scale):
     spread, total = jaa - jbb, jaa + jbb
@@ -223,7 +262,7 @@
     return top / ((p + q + 0.1 * (dh * dv)) * (ah * av))
 
 
-def vertical_kernel(gray_ref, low_ref, high_ref, hor_ref, out_ref, sums):
+def outer_kernel(gray_ref, low_ref, high_ref, hor_ref, inner_ref, out_ref, sums, depth):
     band, last = lax.axis_index("band"), lax.axis_size("band") - 1
     has_low = jnp.where(band > 0, F32(1.0), F32(0.0))
     has_high = jnp.where(band < last, F32(1.0), F32(0.0))
@@ -234,38 +273,26 @@
         return gray_ref[s, r] if r < 16 else high_ref[r - 16, s].astype(F32)
 
     for s in range(16):
-        smoothers = [Smoother() for _ in range(3)]
-        for q in range(20):
-            r = q - 2
-            if s == 0:
-                grad_cam = -field(1, r)
-            elif s == 15:
-                grad_cam = field(14, r)
-            else:
-                grad_cam = field(s - 1, r) - field(s + 1, r)
-            grad_img = field(s, r + 1) - field(s, r - 1)
-            if r < 0:
-                grad_img = grad_img * has_low
-            if r >= 16:
-                grad_img = grad_img * has_high
-            products = (grad_cam * grad_cam, grad_cam * grad_img, grad_img * grad_img)
-            for f in range(3):
-                value = smoothers[f].push(products[f])
-                if q >= 4:
-                    sums[f, s, pl.ds(q - 4, 16, stride=PITCH), :] = value
-
-    for t in range(16):
-        smoothers = [Smoother() for _ in range(3)]
-        for s in range(18):
-            vertical = [
-                smoothers[f].push(sums[f, s, t * PITCH : t * PITCH + 16, :] if s < 16 else None)
-                for f in range(3)
-            ]
-            if s >= 2:
-                c, i = (s - 2) // 2, (s - 2) % 2
-                horizontal = [hor_ref[f, s - 2, t * 16 : (t + 1) * 16, :] for f in range(3)]
-                rows = slice(t % 4 * 16, t % 4 * 16 + 16)
-                out_ref[c, t // 4, i, rows, :] = merge(horizontal, vertical).astype(BF16)
+        for side in range(2):
+            smoothers = [Smoother() for _ in range(3)]
+            for q in range(7):
+                r = q + 11 if side else q - 2
+                factor = has_low if r < 0 else has_high if r >= 16 else None
+                products = products_of(field, s, r, factor)
+                for f in range(3):
+                    value = smoothers[f].push(products[f])
+                    if q >= 4:
+                        sums[f, s, side * 3 + q - 4] = value
+    merge_rows((0, 1, 2, 13, 14, 15), sums, hor_ref, depth)
+
+    row = iota((16, LANES), 0)
+    is_inner = (row >= 3) & (row < 13)
+    for s in range(16):
+        for t in range(16):
+            lines = slice(t * PITCH, t * PITCH + 16)
+            value = jnp.where(is_inner, inner_ref[s, lines, :], depth[s, lines, :])
+            rows = slice(t % 4 * 16, t % 4 * 16 + 16)
+            out_ref[s // 2, t // 4, s % 2, rows, :] = value.astype(BF16)
 
 
 def spread_kernel(chunks, in_ref, out_ref, scratch, sent):
@@ -293,7 +320,7 @@
         functools.partial(gray_kernel, chunks),
         in_specs=[hbm, hbm],
         out_specs=vmem,
-        out_shape=jax.ShapeDtypeStruct((chunks, 144, LANES), BF16),
+        out_shape=jax.ShapeDtypeStruct((chunks, 136, LANES), BF16),
         scratch_shapes=[
             pltpu.VMEM((8, 4, 16, chunks * LANES), BF16),
             pltpu.VMEM((chunks + 2, 16, LANES), F32),
@@ -304,7 +331,7 @@
         compiler_params=params(58),
         name="gray",
     )(channel_weights, light_field)
-    columns = lax.all_to_all(packed, group, 0, 0, tiled=True).reshape(8, 4, 144, LANES)
+    columns = lax.all_to_all(packed, group, 0, 0, tiled=True).reshape(8, 4, 136, LANES)
 
     first, final = pl.pallas_call(
         edges_kernel,
@@ -318,13 +345,14 @@
     low = lax.ppermute(final, "band", [(n, n + 1) for n in range(bands - 1)])
     high = lax.ppermute(first, "band", [(n + 1, n) for n in range(bands - 1)])
 
-    hor, gray = pl.pallas_call(
-        horizontal_kernel,
+    hor, gray, inner = pl.pallas_call(
+        inner_kernel,
         in_specs=[vmem],
-        out_specs=[vmem, vmem],
+        out_specs=[vmem, vmem, vmem],
         out_shape=[
-            jax.ShapeDtypeStruct((3, 16, 256, LANES), F32),
+            jax.ShapeDtypeStruct((3, 16, 16 * PITCH, LANES), F32),
             jax.ShapeDtypeStruct((16, 16, 16, LANES), F32),
+            jax.ShapeDtypeStruct((16, 16 * PITCH, LANES), F32),
         ],
         scratch_shapes=[
             pltpu.VMEM((2, 256, LANES), BF16),
@@ -332,21 +360,25 @@
             pltpu.VMEM((8, 256, LANES), BF16),
             pltpu.VMEM((8, 256, LANES), BF16),
             pltpu.VMEM((16, 16 * PITCH, LANES), F32),
+            pltpu.VMEM((3, 16, 10, 16, LANES), F32),
         ],
-        compiler_params=params(24),
+        compiler_params=params(28),
         cost_estimate=pl.CostEstimate(flops=10**9, bytes_accessed=8 * MIB, transcendentals=0),
-        name="horizontal",
+        name="inner",
     )(columns)
 
     depth = pl.pallas_call(
-        vertical_kernel,
-        in_specs=[vmem, vmem, vmem, vmem],
+        outer_kernel,
+        in_specs=[vmem] * 5,
         out_specs=vmem,
         out_shape=jax.ShapeDtypeStruct((8, 4, 2, 64, LANES), BF16),
-        scratch_shapes=[pltpu.VMEM((3, 16, 16 * PITCH, LANES), F32)],
-        compiler_params=params(24),
-        name="vertical",
-    )(gray, low, high, hor)
+        scratch_shapes=[
+            pltpu.VMEM((3, 16, 6, 16, LANES), F32),
+            pltpu.VMEM((16, 16 * PITCH, LANES), F32),
+        ],
+        compiler_params=params(28),
+        name="outer",
+    )(gray, low, high, hor, inner)
 
     back = lax.all_to_all(depth.reshape(chunks, 128, LANES), group, 0, 0, tiled=True)
     out = pl.pallas_call(

time: 71.2 us -> 68.3 us (0.959)
  waiting for transfers between devices: 2.27 us -> 0.04 us
    ppermute x1, waiting for transfers between devices: 2.27 us -> 0.04 us  [per_device(): high = lax.ppermute(first, 'band', [(n + 1, n) for n in range(bands - 1)])]
  transfers between devices with their start and end apart: 2 -> 2, of which waited for: 1 -> 0; matrix products, arithmetic and copies ran while one was open for 0% -> 0% of each run, Pallas kernels for 5% -> 8%
where the time goes in v2:
time: 68.3 us; the launch traced here: 67.1 us
  blocking collectives  48.5 us (71%)
  Pallas kernels  13.3 us (19%)
  starting transfers between devices  5.29 us (8%)
    all_to_all x1, blocking collectives, per_device(): lax.all_to_all(packed, group, 0, 0, tiled=True).reshape(8, 4, 136, LANES)  27 us
    all_to_all x1, blocking collectives, per_device(): lax.all_to_all(depth.reshape(chunks, 128, LANES), group, 0, 0, tiled=True)  21.5 us
    pallas_call x1, Pallas kernels, per_device(): pl.pallas_call(inner_kernel, in_specs=[vmem], out_specs=[vmem, vmem, vmem...  5.51 us
    pallas_call x1, Pallas kernels, per_device(): pl.pallas_call(functools.partial(gray_kernel, chunks), in_specs=[hbm, hbm...  3.98 us
    ppermute x1, starting transfers between devices, per_device(): low = lax.ppermute(final, 'band', [(n, n + 1) for n in range(bands - 1)])  3.2 us
    pallas_call x1, Pallas kernels, per_device(): pl.pallas_call(outer_kernel, in_specs=[vmem] * 5, out_specs=vmem, out_sha...  2.16 us
    ppermute x1, starting transfers between devices, per_device(): high = lax.ppermute(first, 'band', [(n + 1, n) for n in range(bands - 1)])  2.09 us
    pallas_call x1, Pallas kernels, per_device(): pl.pallas_call(functools.partial(spread_kernel, chunks), in_specs=[vmem],...  1.39 us
  transfers between devices with their start and end apart: 2, of which 0 were waited for; matrix products, arithmetic and copies ran while one was open for 0% of the time, Pallas kernels for 8%

profile of v2, /device:TPU:9, one launch (start us, length us, event | category | flops | bytes accessed | tf_op | source)
XLA Modules:
  0.0 67.1 jit_solution(2502160476142991230)
XLA Ops:
  0.0 4.0 %gray.1 = bf16[32,136,128]{2,1,0:T(8,128)(2,1)} custom-call(f32[4]{0:T(128)} %weights_hbm.1, bf16[4,2,4,16,4096]{4,3,2,1,0:T(8,128)(2,1)} %field_ref.1), custom_call_target="tpu_custom_call" | custom-call | tf_op jit(solution)/shard_map/gray/pallas_call | solution.py:319
  4.0 27.0 %all_to_all.10 = bf16[32,136,128]{2,1,0:T(8,128)(2,1)S(1)} all-to-all(bf16[32,136,128]{2,1,0:T(8,128)(2,1)} %gray.1), channel_id=1, replica_groups=mesh['crow'=8,'ccol'=4,'band'=4] {'crow','ccol'}, dimensions={0} | all-to-all | bytes 2228224 | tf_op jit(solution)/shard_map/all_to_all | solution.py:334
  31.0 0.2 edges.1
  31.2 3.2 %collective-permute-start = (bf16[3,16,16,128]{3,2,1,0:T(8,128)(2,1)S(1)}, bf16[3,16,16,128]{3,2,1,0:T(8,128)(2,1)S(1)}, u32[]{:S(2)}, u32[]{:S(2)}) collective-permute-start(bf16[3,16,16,128]{3,2,1,0:T(8,128)(2,1)S(1)} %get-tuple-element.11), channel_id=1, source_target_pairs={{0,1},{1,2},{2,3},{4,5},{5,6},{6,7},{8,9},{9,10},{10,11},{12,13},{... | collective-permute-start | bytes 589832 | tf_op jit(solution)/shard_map/ppermute | solution.py:345
  34.5 2.1 %collective-permute-start.1 = (bf16[3,16,16,128]{3,2,1,0:T(8,128)(2,1)S(1)}, bf16[3,16,16,128]{3,2,1,0:T(8,128)(2,1)S(1)}, u32[]{:S(2)}, u32[]{:S(2)}) collective-permute-start(bf16[3,16,16,128]{3,2,1,0:T(8,128)(2,1)S(1)} %get-tuple-element.12), channel_id=1, source_target_pairs={{1,0},{2,1},{3,2},{5,4},{6,5},{7,6},{9,8},{10,9},{11,10},{13,12},{... | collective-permute-start | bytes 589832 | tf_op jit(solution)/shard_map/ppermute | solution.py:346
  36.5 5.5 %inner.1 = (f32[3,16,272,128]{3,2,1,0:T(8,128)S(1)}, f32[16,16,16,128]{3,2,1,0:T(8,128)S(1)}, f32[16,272,128]{2,1,0:T(8,128)S(1)}) custom-call(bf16[8,4,136,128]{3,2,1,0:T(8,128)(2,1)S(1)} %bitcast.4), custom_call_target="tpu_custom_call" | custom-call | flops 1000000000 | bytes 8388608 | tf_op jit(solution)/shard_map/inner/pallas_call | solution.py:348
  42.1 0.0 collective-permute-done.low_ref
  42.1 0.0 collective-permute-done.1.high_ref
  42.1 2.2 %outer.1 = bf16[8,4,2,64,128]{4,3,2,1,0:T(8,128)(2,1)S(1)} custom-call(f32[16,16,16,128]{3,2,1,0:T(8,128)S(1)} %get-tuple-element.10.gray_ref, bf16[3,16,16,128]{3,2,1,0:T(8,128)(2,1)S(1)} %collective-permute-done.low_ref, bf16[3,16,16,128]{3,2,1,0:T(8,128)(2,1)S(1)} %collective-permute-done.1.high_ref, f32[3,16,272,128]{3,2,1,0:T(8,128)S(1)} %get-tuple-element.13.hor_ref, ...), custom_call_target="tpu_custom_call" | custom-call | tf_op jit(solution)/shard_map/outer/pallas_call | solution.py:370
  44.3 21.5 %all_to_all.11.in_ref = bf16[32,128,128]{2,1,0:T(8,128)(2,1)S(1)} all-to-all(bf16[32,128,128]{2,1,0:T(8,128)(2,1)S(1)} %bitcast.5), channel_id=1, replica_groups=mesh['crow'=8,'ccol'=4,'band'=4] {'crow','ccol'}, dimensions={0} | all-to-all | bytes 2097152 | tf_op jit(solution)/shard_map/all_to_all | solution.py:383
  65.8 1.4 %spread.1 = f32[128,4096]{1,0:T(8,128)} custom-call(bf16[32,128,128]{2,1,0:T(8,128)(2,1)S(1)} %all_to_all.11.in_ref), custom_call_target="tpu_custom_call" | custom-call | tf_op jit(solution)/shard_map/spread/pallas_call | solution.py:384
Async XLA Ops:
  31.2 10.8 %collective-permute-start = (bf16[3,16,16,128]{3,2,1,0:T(8,128)(2,1)S(1)}, bf16[3,16,16,128]{3,2,1,0:T(8,128)(2,1)S(1)}, u32[]{:S(2)}, u32[]{:S(2)}) collective-permute-start(bf16[3,16,16,128]{3,2,1,0:T(8,128)(2,1)S(1)} %get-tuple-element.11), channel_id=1, source_target_pairs={{0,1},{1,2},{2,3},{4,5},{5,6},{6,7},{8,9},{9,10},{10,11},{12,13},{... | collective-permute-start | bytes 589832 | tf_op jit(solution)/shard_map/ppermute | solution.py:345
  34.5 7.7 %collective-permute-start.1 = (bf16[3,16,16,128]{3,2,1,0:T(8,128)(2,1)S(1)}, bf16[3,16,16,128]{3,2,1,0:T(8,128)(2,1)S(1)}, u32[]{:S(2)}, u32[]{:S(2)}) collective-permute-start(bf16[3,16,16,128]{3,2,1,0:T(8,128)(2,1)S(1)} %get-tuple-element.12), channel_id=1, source_target_pairs={{1,0},{2,1},{3,2},{5,4},{6,5},{7,6},{9,8},{10,9},{11,10},{13,12},{... | collective-permute-start | bytes 589832 | tf_op jit(solution)/shard_map/ppermute | solution.py:346

commit v3 on v2

--- a/solution.py
+++ b/solution.py
@@ -25,51 +25,70 @@
     return total
 
 
-def gray_kernel(chunks, weights_hbm, field_ref, out_ref, field, edges, weights_ref, arrived, known):
-    def incoming(cam):
-        return pltpu.make_async_copy(
-            field_ref.at[:, cam // 4, cam % 4], field.at[cam], arrived.at[cam]
-        )
-
+PIECE = 4
+
+
+def gray_kernel(chunks, weights_hbm, field_ref, out_ref, field, packed, weights_ref, arrived, sent, known):
     weights_copy = pltpu.make_async_copy(weights_hbm, weights_ref, known)
     weights_copy.start()
-    for cam in range(8):
-        incoming(cam).start()
+    pieces = chunks // PIECE
+    copies = []
+    for piece in range(pieces):
+        lanes = pl.ds(piece * PIECE * LANES, PIECE * LANES)
+        copies.append(
+            pltpu.make_async_copy(
+                field_ref.at[:, :, :, :, lanes], field.at[piece], arrived.at[piece]
+            )
+        )
+        copies[-1].start()
     row, lane = iota((16, LANES), 0), iota((16, LANES), 1)
     wanted = jnp.where(row < 3, row + 125, jnp.where(row == 3, 0, jnp.where(row == 4, 127, row - 5)))
     select = jnp.where((row < 8) & (lane == wanted), F32(1.0), F32(0.0)).astype(BF16)
-    edges[0] = jnp.zeros((16, LANES), F32)
-    edges[chunks + 1] = jnp.zeros((16, LANES), F32)
+    low, middle = row < 3, row < 5
     weights_copy.wait()
     weights = [weights_ref[channel] for channel in range(4)]
-
-    @pl.loop(0, 8)
-    def _(cam):
-        incoming(cam).wait()
-        rows = pl.ds(pl.multiple_of(cam * 16, 16), 16)
-        for chunk in range(chunks):
-            lanes = slice(chunk * LANES, (chunk + 1) * LANES)
-            total = field[cam, 0, :, lanes].astype(F32) * weights[0]
-            for channel in range(1, 4):
-                total = total + field[cam, channel, :, lanes].astype(F32) * weights[channel]
-            out_ref[chunk, rows, :] = total.astype(BF16)
-
-    @pl.loop(0, chunks, unroll=32)
-    def _(chunk):
-        edges[chunk + 1] = lax.dot_general(
-            select, out_ref[chunk, 0:128, :], NT, preferred_element_type=F32
-        )
-
-    @pl.loop(0, chunks, unroll=32)
-    def _(chunk):
-        halo = jnp.where(row < 3, edges[chunk], jnp.where(row < 5, edges[chunk + 1], edges[chunk + 2]))
-        out_ref[chunk, 128:136, :] = halo[0:8].astype(BF16)
+    edges = [jnp.zeros((16, LANES), F32)]
+    leaving, done = [], 0
+    for piece in range(pieces):
+        copies[piece].wait()
+        for local in range(PIECE):
+            chunk = piece * PIECE + local
+            lanes = slice(local * LANES, (local + 1) * LANES)
+            levels = []
+            for cam in range(8):
+                total = field[piece, 0, cam // 4, cam % 4, :, lanes].astype(F32) * weights[0]
+                for channel in range(1, 4):
+                    value = field[piece, channel, cam // 4, cam % 4, :, lanes]
+                    total = total + value.astype(F32) * weights[channel]
+                levels.append(total.astype(BF16))
+            levels = jnp.concatenate(levels)
+            packed[chunk, 0:128, :] = levels
+            edges.append(lax.dot_general(select, levels, NT, preferred_element_type=F32))
+        if piece == pieces - 1:
+            edges.append(edges[0])
+        ready = len(edges) - 2
+        for chunk in range(done, ready):
+            left, own, right = edges[chunk : chunk + 3]
+            halo = jnp.where(low, left, jnp.where(middle, own, right))
+            packed[chunk, 128:136, :] = halo[0:8].astype(BF16)
+        part = pl.ds(done, ready - done)
+        leaving.append(pltpu.make_async_copy(packed.at[part], out_ref.at[part], sent.at[piece]))
+        leaving[-1].start()
+        done = ready
+    for copy in leaving:
+        copy.wait()
 
 
 PITCH = 17
 
 
-def edges_kernel(in_ref, first_ref, last_ref, scratch):
+def is_first_core():
+    return lax.rem(lax.axis_index("ccol"), 2) == 0
+
+
+def edges_kernel(in_ref, up_ref, down_ref, scratch):
+    up = jnp.where(is_first_core(), 13, 0)
+    down = 13 - up
     for c in range(8):
         for i in range(2):
             s = c * 2 + i
@@ -77,8 +96,8 @@
                 rows = slice(i * 64 + t % 4 * 16, i * 64 + t % 4 * 16 + 16)
                 scratch[s, t * PITCH : t * PITCH + 16, :] = in_ref[c, t // 4, rows, :].astype(F32)
             for r in range(3):
-                first_ref[r, s] = scratch[s, pl.ds(r, 16, stride=PITCH), :].astype(BF16)
-                last_ref[r, s] = scratch[s, pl.ds(r + 13, 16, stride=PITCH), :].astype(BF16)
+                up_ref[r, s] = scratch[s, pl.ds(r + up, 16, stride=PITCH), :].astype(BF16)
+                down_ref[r, s] = scratch[s, pl.ds(r + down, 16, stride=PITCH), :].astype(BF16)
 
 
 class Smoother:
@@ -142,30 +161,10 @@
                 depth_ref[s - 2, lines, :] = merge(horizontal, vertical)
 
 
-def inner_kernel(
-    in_ref, out_ref, gray_ref, depth_ref, edge, edge_sums, grads, smooths, scratch, sums
-):
+def matrices_kernel(grads, smooths):
     k, u = iota((LANES, LANES), 0), iota((LANES, LANES), 1)
     d = k - u
     dist = jnp.abs(d)
-    eye = ones_where((d == 0, 1.0)).astype(BF16)
-    for col in range(4):
-        rows = [in_ref[c, col, 128:136, :].astype(F32) for c in range(8)]
-        rows = jnp.concatenate(rows + [jnp.zeros((64, LANES), F32)]).astype(BF16)
-        moved = lax.dot_general(eye, rows, NT, preferred_element_type=F32).astype(BF16)
-        for i in range(2):
-            edge[i, col * 64 : (col + 1) * 64, :] = moved[i * 64 : (i + 1) * 64]
-    slot = u & 7
-    used = ((k >> 3) == (u >> 3)) & ((slot == 1) | (slot == 2) | (slot == 5) | (slot == 6))
-    grad = ones_where((used & (d == 1), 1.0), (used & (d == -1), -1.0)).astype(BF16)
-    for i in range(2):
-        values = edge[i]
-        grad_img = jnp.dot(values, grad, preferred_element_type=F32)
-        summed = tensor_of_cameras(split(values.astype(F32)), split(grad_img))
-        for f in range(3):
-            for t in range(16):
-                edge_sums[f, i, t * 16 : (t + 1) * 16, :] = summed[f][t]
-
     group = ("crow", "ccol")
     place, last = lax.axis_index(group), lax.axis_size(group) - 1
     unit = 1.0 / 1024.0
@@ -194,6 +193,30 @@
                 pair = [side if n * 2 + m == c else zero for m in range(2)]
                 matrix[c, 128 + n * 16 : 144 + n * 16, :] = jnp.concatenate(pair).astype(BF16)
 
+
+def inner_kernel(
+    in_ref, grads, smooths, out_ref, gray_ref, depth_ref, edge, edge_sums, scratch, sums
+):
+    k, u = iota((LANES, LANES), 0), iota((LANES, LANES), 1)
+    d = k - u
+    eye = ones_where((d == 0, 1.0)).astype(BF16)
+    for col in range(4):
+        rows = [in_ref[c, col, 128:136, :].astype(F32) for c in range(8)]
+        rows = jnp.concatenate(rows + [jnp.zeros((64, LANES), F32)]).astype(BF16)
+        moved = lax.dot_general(eye, rows, NT, preferred_element_type=F32).astype(BF16)
+        for i in range(2):
+            edge[i, col * 64 : (col + 1) * 64, :] = moved[i * 64 : (i + 1) * 64]
+    slot = u & 7
+    used = ((k >> 3) == (u >> 3)) & ((slot == 1) | (slot == 2) | (slot == 5) | (slot == 6))
+    grad = ones_where((used & (d == 1), 1.0), (used & (d == -1), -1.0)).astype(BF16)
+    for i in range(2):
+        values = edge[i]
+        grad_img = jnp.dot(values, grad, preferred_element_type=F32)
+        summed = tensor_of_cameras(split(values.astype(F32)), split(grad_img))
+        for f in range(3):
+            for t in range(16):
+                edge_sums[f, i, t * 16 : (t + 1) * 16, :] = summed[f][t]
+
     def values_of(c, i):
         return in_ref[c, :, i * 64 : (i + 1) * 64, :].reshape(256, LANES)
 
@@ -262,15 +285,22 @@
     return top / ((p + q + 0.1 * (dh * dv)) * (ah * av))
 
 
-def outer_kernel(gray_ref, low_ref, high_ref, hor_ref, inner_ref, out_ref, sums, depth):
+def outer_kernel(gray_ref, one_ref, two_ref, hor_ref, inner_ref, out_ref, sums, depth, halo):
     band, last = lax.axis_index("band"), lax.axis_size("band") - 1
     has_low = jnp.where(band > 0, F32(1.0), F32(0.0))
     has_high = jnp.where(band < last, F32(1.0), F32(0.0))
 
+    first_core = is_first_core()
+    for r in range(3):
+        for s in range(16):
+            one, two = one_ref[r, s].astype(F32), two_ref[r, s].astype(F32)
+            halo[r, s] = jnp.where(first_core, one, two)
+            halo[r + 3, s] = jnp.where(first_core, two, one)
+
     def field(s, r):
         if r < 0:
-            return low_ref[r + 3, s].astype(F32)
-        return gray_ref[s, r] if r < 16 else high_ref[r - 16, s].astype(F32)
+            return halo[r + 3, s]
+        return gray_ref[s, r] if r < 16 else halo[r - 13, s]
 
     for s in range(16):
         for side in range(2):
@@ -319,21 +349,31 @@
     packed = pl.pallas_call(
         functools.partial(gray_kernel, chunks),
         in_specs=[hbm, hbm],
-        out_specs=vmem,
+        out_specs=hbm,
         out_shape=jax.ShapeDtypeStruct((chunks, 136, LANES), BF16),
         scratch_shapes=[
-            pltpu.VMEM((8, 4, 16, chunks * LANES), BF16),
-            pltpu.VMEM((chunks + 2, 16, LANES), F32),
+            pltpu.VMEM((chunks // PIECE, 4, 2, 4, 16, PIECE * LANES), BF16),
+            pltpu.VMEM((chunks, 136, LANES), BF16),
             pltpu.SMEM((4,), F32),
-            pltpu.SemaphoreType.DMA((8,)),
+            pltpu.SemaphoreType.DMA((chunks // PIECE,)),
+            pltpu.SemaphoreType.DMA((chunks // PIECE,)),
             pltpu.SemaphoreType.DMA,
         ],
         compiler_params=params(58),
         name="gray",
     )(channel_weights, light_field)
     columns = lax.all_to_all(packed, group, 0, 0, tiled=True).reshape(8, 4, 136, LANES)
-
-    first, final = pl.pallas_call(
+    grads, smooths = pl.pallas_call(
+        matrices_kernel,
+        out_specs=[vmem, vmem],
+        out_shape=[jax.ShapeDtypeStruct((8, 256, LANES), BF16)] * 2,
+        compiler_params=params(8),
+        cost_estimate=pl.CostEstimate(flops=10**9, bytes_accessed=8 * MIB, transcendentals=0),
+        name="matrices",
+    )()
+    columns, grads, smooths = lax.optimization_barrier((columns, grads, smooths))
+
+    ahead, behind = pl.pallas_call(
         edges_kernel,
         in_specs=[vmem],
         out_specs=[vmem, vmem],
@@ -342,12 +382,14 @@
         compiler_params=params(16),
         name="edges",
     )(columns)
-    low = lax.ppermute(final, "band", [(n, n + 1) for n in range(bands - 1)])
-    high = lax.ppermute(first, "band", [(n + 1, n) for n in range(bands - 1)])
+    pairs = [(k % 2, k * bands + n, k * bands + n + 1) for k in range(4) for n in range(bands - 1)]
+    both = ("ccol", "band")
+    one = lax.ppermute(ahead, both, [(b, a) if odd else (a, b) for odd, a, b in pairs])
+    two = lax.ppermute(behind, both, [(a, b) if odd else (b, a) for odd, a, b in pairs])
 
     hor, gray, inner = pl.pallas_call(
         inner_kernel,
-        in_specs=[vmem],
+        in_specs=[vmem, vmem, vmem],
         out_specs=[vmem, vmem, vmem],
         out_shape=[
             jax.ShapeDtypeStruct((3, 16, 16 * PITCH, LANES), F32),
@@ -357,15 +399,13 @@
         scratch_shapes=[
             pltpu.VMEM((2, 256, LANES), BF16),
             pltpu.VMEM((3, 2, 256, LANES), BF16),
-            pltpu.VMEM((8, 256, LANES), BF16),
-            pltpu.VMEM((8, 256, LANES), BF16),
             pltpu.VMEM((16, 16 * PITCH, LANES), F32),
             pltpu.VMEM((3, 16, 10, 16, LANES), F32),
         ],
         compiler_params=params(28),
         cost_estimate=pl.CostEstimate(flops=10**9, bytes_accessed=8 * MIB, transcendentals=0),
         name="inner",
-    )(columns)
+    )(columns, grads, smooths)
 
     depth = pl.pallas_call(
         outer_kernel,
@@ -375,10 +415,11 @@
         scratch_shapes=[
             pltpu.VMEM((3, 16, 6, 16, LANES), F32),
             pltpu.VMEM((16, 16 * PITCH, LANES), F32),
+            pltpu.VMEM((6, 16, 16, LANES), F32),
         ],
         compiler_params=params(28),
         name="outer",
-    )(gray, low, high, hor, inner)
+    )(gray, one, two, hor, inner)
 
     back = lax.all_to_all(depth.reshape(chunks, 128, LANES), group, 0, 0, tiled=True)
     out = pl.pallas_call(

time: 68.3 us -> 66.6 us (0.975)
  blocking collectives: 48.5 us -> 21.2 us
  waiting for transfers between devices: 0.04 us -> 17.5 us
  starting transfers between devices: 5.29 us -> 13.9 us
    all_to_all x1 -> x0, blocking collectives: 27 us -> none  [per_device(): lax.all_to_all(packed, group, 0, 0, tiled=True).reshape(8, 4, 136, LANES)]
    all_to_all x0 -> x1, waiting for transfers between devices: none -> 17.5 us  [per_device(): lax.all_to_all(packed, group, 0, 0, tiled=True).reshape(8, 4, 136, LANES)]
    all_to_all x0 -> x1, starting transfers between devices: none -> 8.61 us  [per_device(): lax.all_to_all(packed, group, 0, 0, tiled=True).reshape(8, 4, 136, LANES)]
    pallas_call x1 -> x2, Pallas kernels: 5.51 us -> 5.55 us  [the longest x1 5.45 us: per_device(): pl.pallas_call(inner_kernel, in_specs=[vmem, vmem, vmem], out_specs=[vmem...]
  transfers between devices with their start and end apart: 2 -> 3, of which waited for: 0 -> 1; matrix products, arithmetic and copies ran while one was open for 0% -> 0% of each run, Pallas kernels for 8% -> 8%
where the time goes in v3:
time: 66.6 us; the launch traced here: 65.8 us
  blocking collectives  21.2 us (32%)
  waiting for transfers between devices  17.5 us (26%)
  starting transfers between devices  13.9 us (21%)
  Pallas kernels  13.1 us (20%)
    all_to_all x1, blocking collectives, per_device(): lax.all_to_all(depth.reshape(chunks, 128, LANES), group, 0, 0, tiled=True)  21.2 us
    all_to_all x1, waiting for transfers between devices, per_device(): lax.all_to_all(packed, group, 0, 0, tiled=True).reshape(8, 4, 136, LANES)  17.5 us
    all_to_all x1, starting transfers between devices, per_device(): lax.all_to_all(packed, group, 0, 0, tiled=True).reshape(8, 4, 136, LANES)  8.61 us
    pallas_call x1, Pallas kernels, per_device(): pl.pallas_call(inner_kernel, in_specs=[vmem, vmem, vmem], out_specs=[vmem...  5.45 us
    pallas_call x1, Pallas kernels, per_device(): pl.pallas_call(functools.partial(gray_kernel, chunks), in_specs=[hbm, hbm...  3.65 us
    ppermute x1, starting transfers between devices, per_device(): lax.ppermute(behind, both, [(a, b) if odd else (b, a) for odd, a, b in pa...  3.2 us
    pallas_call x1, Pallas kernels, per_device(): pl.pallas_call(outer_kernel, in_specs=[vmem] * 5, out_specs=vmem, out_sha...  2.2 us
    ppermute x1, starting transfers between devices, per_device(): lax.ppermute(ahead, both, [(b, a) if odd else (a, b) for odd, a, b in pai...  2.08 us
  transfers between devices with their start and end apart: 3, of which 1 were waited for; matrix products, arithmetic and copies ran while one was open for 0% of the time, Pallas kernels for 8%

profile of v3, /device:TPU:9, one launch (start us, length us, event | category | flops | bytes accessed | tf_op | source)
XLA Modules:
  0.0 65.8 jit_solution(10724412643442075622)
XLA Ops:
  0.0 3.6 %gray.1 = bf16[32,136,128]{2,1,0:T(8,128)(2,1)} custom-call(f32[4]{0:T(128)} %weights_hbm.1, bf16[4,2,4,16,4096]{4,3,2,1,0:T(8,128)(2,1)} %field_ref.1), custom_call_target="tpu_custom_call" | custom-call | tf_op jit(solution)/shard_map/gray/pallas_call | solution.py:349
  3.7 8.6 %all-to-all-start = ((bf16[32,136,128]{2,1,0:T(8,128)(2,1)}), bf16[32,136,128]{2,1,0:T(8,128)(2,1)S(1)}, u32[]{:S(2)}, u32[]{:S(2)}) async-start(bf16[32,136,128]{2,1,0:T(8,128)(2,1)} %gray.1), calls=%async_computation | async-start | bytes 2228224 | tf_op jit(solution)/shard_map/all_to_all | solution.py:365
  12.3 0.1 matrices.1
  12.4 17.5 %all-to-all-done = bf16[32,136,128]{2,1,0:T(8,128)(2,1)S(1)} async-done(((bf16[32,136,128]{2,1,0:T(8,128)(2,1)}), bf16[32,136,128]{2,1,0:T(8,128)(2,1)S(1)}, u32[]{:S(2)}, u32[]{:S(2)}) %all-to-all-start) | async-done | bytes 1114144 | tf_op jit(solution)/shard_map/all_to_all | solution.py:365
  29.9 0.3 edges.1
  30.2 2.1 %collective-permute-start = (bf16[3,16,16,128]{3,2,1,0:T(8,128)(2,1)S(1)}, bf16[3,16,16,128]{3,2,1,0:T(8,128)(2,1)S(1)}, u32[]{:S(2)}, u32[]{:S(2)}) collective-permute-start(bf16[3,16,16,128]{3,2,1,0:T(8,128)(2,1)S(1)} %get-tuple-element.21), channel_id=1, source_target_pairs={{0,1},{1,2},{2,3},{5,4},{6,5},{7,6},{8,9},{9,10},{10,11},{13,12},{... | collective-permute-start | bytes 589832 | tf_op jit(solution)/shard_map/ppermute | solution.py:387
  32.3 3.2 %collective-permute-start.1 = (bf16[3,16,16,128]{3,2,1,0:T(8,128)(2,1)S(1)}, bf16[3,16,16,128]{3,2,1,0:T(8,128)(2,1)S(1)}, u32[]{:S(2)}, u32[]{:S(2)}) collective-permute-start(bf16[3,16,16,128]{3,2,1,0:T(8,128)(2,1)S(1)} %get-tuple-element.22), channel_id=1, source_target_pairs={{1,0},{2,1},{3,2},{4,5},{5,6},{6,7},{9,8},{10,9},{11,10},{12,13},{... | collective-permute-start | bytes 589832 | tf_op jit(solution)/shard_map/ppermute | solution.py:388
  35.5 5.4 %inner.1 = (f32[3,16,272,128]{3,2,1,0:T(8,128)S(1)}, f32[16,16,16,128]{3,2,1,0:T(8,128)S(1)}, f32[16,272,128]{2,1,0:T(8,128)S(1)}) custom-call(bf16[8,4,136,128]{3,2,1,0:T(8,128)(2,1)S(1)} %bitcast.4, bf16[8,256,128]{2,1,0:T(8,128)(2,1)S(1)} %get-tuple-element.18.grads, bf16[8,256,128]{2,1,0:T(8,128)(2,1)S(1)} %get-tuple-element.19.smooths), custom_call_target="tpu_custom_call" | custom-call | flops 1000000000 | bytes 8388608 | tf_op jit(solution)/shard_map/inner/pallas_call | solution.py:390
  40.9 0.0 collective-permute-done.one_ref
  40.9 0.0 collective-permute-done.1.two_ref
  41.0 2.2 %outer.1 = bf16[8,4,2,64,128]{4,3,2,1,0:T(8,128)(2,1)S(1)} custom-call(f32[16,16,16,128]{3,2,1,0:T(8,128)S(1)} %get-tuple-element.20.gray_ref, bf16[3,16,16,128]{3,2,1,0:T(8,128)(2,1)S(1)} %collective-permute-done.one_ref, bf16[3,16,16,128]{3,2,1,0:T(8,128)(2,1)S(1)} %collective-permute-done.1.two_ref, f32[3,16,272,128]{3,2,1,0:T(8,128)S(1)} %get-tuple-element.23.hor_ref, ...), custom_call_target="tpu_custom_call" | custom-call | tf_op jit(solution)/shard_map/outer/pallas_call | solution.py:410
  43.2 21.2 %all_to_all.10.in_ref = bf16[32,128,128]{2,1,0:T(8,128)(2,1)S(1)} all-to-all(bf16[32,128,128]{2,1,0:T(8,128)(2,1)S(1)} %bitcast.5), channel_id=1, replica_groups=mesh['crow'=8,'ccol'=4,'band'=4] {'crow','ccol'}, dimensions={0} | all-to-all | bytes 2097152 | tf_op jit(solution)/shard_map/all_to_all | solution.py:424
  64.4 1.4 %spread.1 = f32[128,4096]{1,0:T(8,128)} custom-call(bf16[32,128,128]{2,1,0:T(8,128)(2,1)S(1)} %all_to_all.10.in_ref), custom_call_target="tpu_custom_call" | custom-call | tf_op jit(solution)/shard_map/spread/pallas_call | solution.py:425
Async XLA Ops:
  3.7 26.3 %all-to-all-start = ((bf16[32,136,128]{2,1,0:T(8,128)(2,1)}), bf16[32,136,128]{2,1,0:T(8,128)(2,1)S(1)}, u32[]{:S(2)}, u32[]{:S(2)}) async-start(bf16[32,136,128]{2,1,0:T(8,128)(2,1)} %gray.1), calls=%async_computation | async-start | bytes 2228224 | tf_op jit(solution)/shard_map/all_to_all | solution.py:365
  30.2 10.8 %collective-permute-start = (bf16[3,16,16,128]{3,2,1,0:T(8,128)(2,1)S(1)}, bf16[3,16,16,128]{3,2,1,0:T(8,128)(2,1)S(1)}, u32[]{:S(2)}, u32[]{:S(2)}) collective-permute-start(bf16[3,16,16,128]{3,2,1,0:T(8,128)(2,1)S(1)} %get-tuple-element.21), channel_id=1, source_target_pairs={{0,1},{1,2},{2,3},{5,4},{6,5},{7,6},{8,9},{9,10},{10,11},{13,12},{... | collective-permute-start | bytes 589832 | tf_op jit(solution)/shard_map/ppermute | solution.py:387
  32.3 8.7 %collective-permute-start.1 = (bf16[3,16,16,128]{3,2,1,0:T(8,128)(2,1)S(1)}, bf16[3,16,16,128]{3,2,1,0:T(8,128)(2,1)S(1)}, u32[]{:S(2)}, u32[]{:S(2)}) collective-permute-start(bf16[3,16,16,128]{3,2,1,0:T(8,128)(2,1)S(1)} %get-tuple-element.22), channel_id=1, source_target_pairs={{1,0},{2,1},{3,2},{4,5},{5,6},{6,7},{9,8},{10,9},{11,10},{12,13},{... | collective-permute-start | bytes 589832 | tf_op jit(solution)/shard_map/ppermute | solution.py:388

commit v4 on v3

--- a/solution.py
+++ b/solution.py
@@ -82,12 +82,12 @@
 PITCH = 17
 
 
-def is_first_core():
-    return lax.rem(lax.axis_index("ccol"), 2) == 0
+def is_even_band():
+    return lax.rem(lax.axis_index("band"), 2) == 0
 
 
 def edges_kernel(in_ref, up_ref, down_ref, scratch):
-    up = jnp.where(is_first_core(), 13, 0)
+    up = jnp.where(is_even_band(), 13, 0)
     down = 13 - up
     for c in range(8):
         for i in range(2):
@@ -290,12 +290,12 @@
     has_low = jnp.where(band > 0, F32(1.0), F32(0.0))
     has_high = jnp.where(band < last, F32(1.0), F32(0.0))
 
-    first_core = is_first_core()
+    even = is_even_band()
     for r in range(3):
         for s in range(16):
             one, two = one_ref[r, s].astype(F32), two_ref[r, s].astype(F32)
-            halo[r, s] = jnp.where(first_core, one, two)
-            halo[r + 3, s] = jnp.where(first_core, two, one)
+            halo[r, s] = jnp.where(even, two, one)
+            halo[r + 3, s] = jnp.where(even, one, two)
 
     def field(s, r):
         if r < 0:
@@ -382,10 +382,11 @@
         compiler_params=params(16),
         name="edges",
     )(columns)
-    pairs = [(k % 2, k * bands + n, k * bands + n + 1) for k in range(4) for n in range(bands - 1)]
-    both = ("ccol", "band")
-    one = lax.ppermute(ahead, both, [(b, a) if odd else (a, b) for odd, a, b in pairs])
-    two = lax.ppermute(behind, both, [(a, b) if odd else (b, a) for odd, a, b in pairs])
+    links = [[(n, n + 1) for n in range(start, bands - 1, 2)] for start in range(2)]
+    one, two = (
+        lax.ppermute(rows, "band", pairs + [(b, a) for a, b in pairs])
+        for rows, pairs in zip((ahead, behind), links)
+    )
 
     hor, gray, inner = pl.pallas_call(
         inner_kernel,

time: 66.6 us -> 65 us (0.976)
  starting transfers between devices: 13.9 us -> 12.9 us
    ppermute x2, starting transfers between devices: 5.28 us -> 4.27 us  [per_device(): lax.ppermute(rows, 'band', pairs + [(b, a) for a, b in pairs])]
  transfers between devices with their start and end apart: 3 -> 3, of which waited for: 1 -> 1; matrix products, arithmetic and copies ran while one was open for 0% -> 0% of each run, Pallas kernels for 8% -> 9%
where the time goes in v4:
time: 65 us; the launch traced here: 64.7 us
  blocking collectives  21.2 us (33%)
  waiting for transfers between devices  17.5 us (27%)
  Pallas kernels  13 us (20%)
  starting transfers between devices  12.9 us (20%)
    all_to_all x1, blocking collectives, per_device(): lax.all_to_all(depth.reshape(chunks, 128, LANES), group, 0, 0, tiled=True)  21.2 us
    all_to_all x1, waiting for transfers between devices, per_device(): lax.all_to_all(packed, group, 0, 0, tiled=True).reshape(8, 4, 136, LANES)  17.5 us
    all_to_all x1, starting transfers between devices, per_device(): lax.all_to_all(packed, group, 0, 0, tiled=True).reshape(8, 4, 136, LANES)  8.61 us
    pallas_call x1, Pallas kernels, per_device(): pl.pallas_call(inner_kernel, in_specs=[vmem, vmem, vmem], out_specs=[vmem...  5.44 us
    ppermute x2, starting transfers between devices, per_device(): lax.ppermute(rows, 'band', pairs + [(b, a) for a, b in pairs])  4.27 us
    pallas_call x1, Pallas kernels, per_device(): pl.pallas_call(functools.partial(gray_kernel, chunks), in_specs=[hbm, hbm...  3.65 us
    pallas_call x1, Pallas kernels, per_device(): pl.pallas_call(outer_kernel, in_specs=[vmem] * 5, out_specs=vmem, out_sha...  2.19 us
    pallas_call x1, Pallas kernels, per_device(): pl.pallas_call(functools.partial(spread_kernel, chunks), in_specs=[vmem],...  1.39 us
  transfers between devices with their start and end apart: 3, of which 1 were waited for; matrix products, arithmetic and copies ran while one was open for 0% of the time, Pallas kernels for 9%

profile of v4, /device:TPU:9, one launch (start us, length us, event | category | flops | bytes accessed | tf_op | source)
XLA Modules:
  0.0 64.7 jit_solution(6088800870847107524)
XLA Ops:
  0.0 3.6 %gray.1 = bf16[32,136,128]{2,1,0:T(8,128)(2,1)} custom-call(f32[4]{0:T(128)} %weights_hbm.1, bf16[4,2,4,16,4096]{4,3,2,1,0:T(8,128)(2,1)} %field_ref.1), custom_call_target="tpu_custom_call" | custom-call | tf_op jit(solution)/shard_map/gray/pallas_call | solution.py:349
  3.7 8.6 %all-to-all-start = ((bf16[32,136,128]{2,1,0:T(8,128)(2,1)}), bf16[32,136,128]{2,1,0:T(8,128)(2,1)S(1)}, u32[]{:S(2)}, u32[]{:S(2)}) async-start(bf16[32,136,128]{2,1,0:T(8,128)(2,1)} %gray.1), calls=%async_computation | async-start | bytes 2228224 | tf_op jit(solution)/shard_map/all_to_all | solution.py:365
  12.3 0.1 matrices.1
  12.4 17.5 %all-to-all-done = bf16[32,136,128]{2,1,0:T(8,128)(2,1)S(1)} async-done(((bf16[32,136,128]{2,1,0:T(8,128)(2,1)}), bf16[32,136,128]{2,1,0:T(8,128)(2,1)S(1)}, u32[]{:S(2)}, u32[]{:S(2)}) %all-to-all-start) | async-done | bytes 1114144 | tf_op jit(solution)/shard_map/all_to_all | solution.py:365
  29.9 0.3 edges.1
  30.2 0.3 collective-permute-start
  30.4 4.0 %collective-permute-start.1 = (bf16[3,16,16,128]{3,2,1,0:T(8,128)(2,1)S(1)}, bf16[3,16,16,128]{3,2,1,0:T(8,128)(2,1)S(1)}, u32[]{:S(2)}, u32[]{:S(2)}) collective-permute-start(bf16[3,16,16,128]{3,2,1,0:T(8,128)(2,1)S(1)} %get-tuple-element.22), channel_id=1, source_target_pairs={{1,2},{2,1},{5,6},{6,5},{9,10},{10,9},{13,14},{14,13},{17,18},{18,... | collective-permute-start | bytes 589832 | tf_op jit(solution)/shard_map/ppermute | solution.py:387
  34.5 5.4 %inner.1 = (f32[3,16,272,128]{3,2,1,0:T(8,128)S(1)}, f32[16,16,16,128]{3,2,1,0:T(8,128)S(1)}, f32[16,272,128]{2,1,0:T(8,128)S(1)}) custom-call(bf16[8,4,136,128]{3,2,1,0:T(8,128)(2,1)S(1)} %bitcast.4, bf16[8,256,128]{2,1,0:T(8,128)(2,1)S(1)} %get-tuple-element.18.grads, bf16[8,256,128]{2,1,0:T(8,128)(2,1)S(1)} %get-tuple-element.19.smooths), custom_call_target="tpu_custom_call" | custom-call | flops 1000000000 | bytes 8388608 | tf_op jit(solution)/shard_map/inner/pallas_call | solution.py:391
  39.9 0.0 collective-permute-done.one_ref
  39.9 0.0 collective-permute-done.1.two_ref
  39.9 2.2 %outer.1 = bf16[8,4,2,64,128]{4,3,2,1,0:T(8,128)(2,1)S(1)} custom-call(f32[16,16,16,128]{3,2,1,0:T(8,128)S(1)} %get-tuple-element.20.gray_ref, bf16[3,16,16,128]{3,2,1,0:T(8,128)(2,1)S(1)} %collective-permute-done.one_ref, bf16[3,16,16,128]{3,2,1,0:T(8,128)(2,1)S(1)} %collective-permute-done.1.two_ref, f32[3,16,272,128]{3,2,1,0:T(8,128)S(1)} %get-tuple-element.23.hor_ref, ...), custom_call_target="tpu_custom_call" | custom-call | tf_op jit(solution)/shard_map/outer/pallas_call | solution.py:411
  42.1 21.2 %all_to_all.10.in_ref = bf16[32,128,128]{2,1,0:T(8,128)(2,1)S(1)} all-to-all(bf16[32,128,128]{2,1,0:T(8,128)(2,1)S(1)} %bitcast.5), channel_id=1, replica_groups=mesh['crow'=8,'ccol'=4,'band'=4] {'crow','ccol'}, dimensions={0} | all-to-all | bytes 2097152 | tf_op jit(solution)/shard_map/all_to_all | solution.py:425
  63.3 1.4 %spread.1 = f32[128,4096]{1,0:T(8,128)} custom-call(bf16[32,128,128]{2,1,0:T(8,128)(2,1)S(1)} %all_to_all.10.in_ref), custom_call_target="tpu_custom_call" | custom-call | tf_op jit(solution)/shard_map/spread/pallas_call | solution.py:426
Async XLA Ops:
  3.7 26.3 %all-to-all-start = ((bf16[32,136,128]{2,1,0:T(8,128)(2,1)}), bf16[32,136,128]{2,1,0:T(8,128)(2,1)S(1)}, u32[]{:S(2)}, u32[]{:S(2)}) async-start(bf16[32,136,128]{2,1,0:T(8,128)(2,1)} %gray.1), calls=%async_computation | async-start | bytes 2228224 | tf_op jit(solution)/shard_map/all_to_all | solution.py:365
  30.2 9.7 %collective-permute-start = (bf16[3,16,16,128]{3,2,1,0:T(8,128)(2,1)S(1)}, bf16[3,16,16,128]{3,2,1,0:T(8,128)(2,1)S(1)}, u32[]{:S(2)}, u32[]{:S(2)}) collective-permute-start(bf16[3,16,16,128]{3,2,1,0:T(8,128)(2,1)S(1)} %get-tuple-element.21), channel_id=1, source_target_pairs={{0,1},{2,3},{1,0},{3,2},{4,5},{6,7},{5,4},{7,6},{8,9},{10,11},{9,8... | collective-permute-start | bytes 589832 | tf_op jit(solution)/shard_map/ppermute | solution.py:387
  30.4 9.5 %collective-permute-start.1 = (bf16[3,16,16,128]{3,2,1,0:T(8,128)(2,1)S(1)}, bf16[3,16,16,128]{3,2,1,0:T(8,128)(2,1)S(1)}, u32[]{:S(2)}, u32[]{:S(2)}) collective-permute-start(bf16[3,16,16,128]{3,2,1,0:T(8,128)(2,1)S(1)} %get-tuple-element.22), channel_id=1, source_target_pairs={{1,2},{2,1},{5,6},{6,5},{9,10},{10,9},{13,14},{14,13},{17,18},{18,... | collective-permute-start | bytes 589832 | tf_op jit(solution)/shard_map/ppermute | solution.py:387

commit v5 on v4

--- a/solution.py
+++ b/solution.py
@@ -239,24 +239,25 @@
         return jnp.concatenate([v for f in range(3) for i in range(2) for v in summed[i][f]])
 
     def smooth(c, parts):
-        side = jnp.concatenate([edge_sums[f, i] for f in range(3) for i in range(2)])
-        full = jnp.dot(
-            jnp.concatenate([parts, side], axis=1), smooths[c], preferred_element_type=F32
-        )
         for f in range(3):
+            own = parts[f * 512 : (f + 1) * 512]
+            side = jnp.concatenate([edge_sums[f, 0], edge_sums[f, 1]])
+            full = jnp.dot(
+                jnp.concatenate([own, side], axis=1), smooths[c], preferred_element_type=F32
+            )
             for i in range(2):
-                n = (f * 2 + i) * 256
                 for t in range(16):
+                    n = i * 256 + t * 16
                     rows = slice(t * PITCH, t * PITCH + 16)
-                    out_ref[f, c * 2 + i, rows, :] = full[n + t * 16 : n + t * 16 + 16]
+                    out_ref[f, c * 2 + i, rows, :] = full[n : n + 16]
 
     grad_img, parts = gradient(0), None
     for c in range(8):
         following = gradient(c + 1) if c < 7 else None
-        now = products(c, grad_img)
         if c:
             smooth(c - 1, parts)
-        grad_img, parts = following, now
+        parts = products(c, grad_img)
+        grad_img = following
     smooth(7, parts)
 
     for s in range(16):

time: 65 us -> 64.6 us (level)
  transfers between devices with their start and end apart: 3 -> 3, of which waited for: 1 -> 1; matrix products, arithmetic and copies ran while one was open for 0% -> 0% of each run, Pallas kernels for 9% -> 8%
where the time goes in v5:
time: 64.6 us; the launch traced here: 64.4 us
  blocking collectives  21.2 us (33%)
  waiting for transfers between devices  17.5 us (27%)
  starting transfers between devices  12.9 us (20%)
  Pallas kernels  12.7 us (20%)
    all_to_all x1, blocking collectives, per_device(): lax.all_to_all(depth.reshape(chunks, 128, LANES), group, 0, 0, tiled=True)  21.2 us
    all_to_all x1, waiting for transfers between devices, per_device(): lax.all_to_all(packed, group, 0, 0, tiled=True).reshape(8, 4, 136, LANES)  17.5 us
    all_to_all x1, starting transfers between devices, per_device(): lax.all_to_all(packed, group, 0, 0, tiled=True).reshape(8, 4, 136, LANES)  8.61 us
    pallas_call x1, Pallas kernels, per_device(): pl.pallas_call(inner_kernel, in_specs=[vmem, vmem, vmem], out_specs=[vmem...  5.05 us
    ppermute x2, starting transfers between devices, per_device(): lax.ppermute(rows, 'band', pairs + [(b, a) for a, b in pairs])  4.27 us
    pallas_call x1, Pallas kernels, per_device(): pl.pallas_call(functools.partial(gray_kernel, chunks), in_specs=[hbm, hbm...  3.65 us
    pallas_call x1, Pallas kernels, per_device(): pl.pallas_call(outer_kernel, in_specs=[vmem] * 5, out_specs=vmem, out_sha...  2.19 us
    pallas_call x1, Pallas kernels, per_device(): pl.pallas_call(functools.partial(spread_kernel, chunks), in_specs=[vmem],...  1.39 us
  transfers between devices with their start and end apart: 3, of which 1 were waited for; matrix products, arithmetic and copies ran while one was open for 0% of the time, Pallas kernels for 8%

profile of v5, /device:TPU:9, one launch (start us, length us, event | category | flops | bytes accessed | tf_op | source)
XLA Modules:
  0.0 64.4 jit_solution(11383698151171676313)
XLA Ops:
  0.0 3.6 %gray.1 = bf16[32,136,128]{2,1,0:T(8,128)(2,1)} custom-call(f32[4]{0:T(128)} %weights_hbm.1, bf16[4,2,4,16,4096]{4,3,2,1,0:T(8,128)(2,1)} %field_ref.1), custom_call_target="tpu_custom_call" | custom-call | tf_op jit(solution)/shard_map/gray/pallas_call | solution.py:350
  3.7 8.6 %all-to-all-start = ((bf16[32,136,128]{2,1,0:T(8,128)(2,1)}), bf16[32,136,128]{2,1,0:T(8,128)(2,1)S(1)}, u32[]{:S(2)}, u32[]{:S(2)}) async-start(bf16[32,136,128]{2,1,0:T(8,128)(2,1)} %gray.1), calls=%async_computation | async-start | bytes 2228224 | tf_op jit(solution)/shard_map/all_to_all | solution.py:366
  12.3 0.1 matrices.1
  12.4 17.5 %all-to-all-done = bf16[32,136,128]{2,1,0:T(8,128)(2,1)S(1)} async-done(((bf16[32,136,128]{2,1,0:T(8,128)(2,1)}), bf16[32,136,128]{2,1,0:T(8,128)(2,1)S(1)}, u32[]{:S(2)}, u32[]{:S(2)}) %all-to-all-start) | async-done | bytes 1114144 | tf_op jit(solution)/shard_map/all_to_all | solution.py:366
  29.9 0.3 edges.1
  30.2 0.3 collective-permute-start
  30.4 4.0 %collective-permute-start.1 = (bf16[3,16,16,128]{3,2,1,0:T(8,128)(2,1)S(1)}, bf16[3,16,16,128]{3,2,1,0:T(8,128)(2,1)S(1)}, u32[]{:S(2)}, u32[]{:S(2)}) collective-permute-start(bf16[3,16,16,128]{3,2,1,0:T(8,128)(2,1)S(1)} %get-tuple-element.22), channel_id=1, source_target_pairs={{1,2},{2,1},{5,6},{6,5},{9,10},{10,9},{13,14},{14,13},{17,18},{18,... | collective-permute-start | bytes 589832 | tf_op jit(solution)/shard_map/ppermute | solution.py:388
  34.5 5.1 %inner.1 = (f32[3,16,272,128]{3,2,1,0:T(8,128)S(1)}, f32[16,16,16,128]{3,2,1,0:T(8,128)S(1)}, f32[16,272,128]{2,1,0:T(8,128)S(1)}) custom-call(bf16[8,4,136,128]{3,2,1,0:T(8,128)(2,1)S(1)} %bitcast.4, bf16[8,256,128]{2,1,0:T(8,128)(2,1)S(1)} %get-tuple-element.18.grads, bf16[8,256,128]{2,1,0:T(8,128)(2,1)S(1)} %get-tuple-element.19.smooths), custom_call_target="tpu_custom_call" | custom-call | flops 1000000000 | bytes 8388608 | tf_op jit(solution)/shard_map/inner/pallas_call | solution.py:392
  39.5 0.0 collective-permute-done.one_ref
  39.5 0.0 collective-permute-done.1.two_ref
  39.6 2.2 %outer.1 = bf16[8,4,2,64,128]{4,3,2,1,0:T(8,128)(2,1)S(1)} custom-call(f32[16,16,16,128]{3,2,1,0:T(8,128)S(1)} %get-tuple-element.20.gray_ref, bf16[3,16,16,128]{3,2,1,0:T(8,128)(2,1)S(1)} %collective-permute-done.one_ref, bf16[3,16,16,128]{3,2,1,0:T(8,128)(2,1)S(1)} %collective-permute-done.1.two_ref, f32[3,16,272,128]{3,2,1,0:T(8,128)S(1)} %get-tuple-element.23.hor_ref, ...), custom_call_target="tpu_custom_call" | custom-call | tf_op jit(solution)/shard_map/outer/pallas_call | solution.py:412
  41.8 21.2 %all_to_all.10.in_ref = bf16[32,128,128]{2,1,0:T(8,128)(2,1)S(1)} all-to-all(bf16[32,128,128]{2,1,0:T(8,128)(2,1)S(1)} %bitcast.5), channel_id=1, replica_groups=mesh['crow'=8,'ccol'=4,'band'=4] {'crow','ccol'}, dimensions={0} | all-to-all | bytes 2097152 | tf_op jit(solution)/shard_map/all_to_all | solution.py:426
  63.0 1.4 %spread.1 = f32[128,4096]{1,0:T(8,128)} custom-call(bf16[32,128,128]{2,1,0:T(8,128)(2,1)S(1)} %all_to_all.10.in_ref), custom_call_target="tpu_custom_call" | custom-call | tf_op jit(solution)/shard_map/spread/pallas_call | solution.py:427
Async XLA Ops:
  3.7 26.3 %all-to-all-start = ((bf16[32,136,128]{2,1,0:T(8,128)(2,1)}), bf16[32,136,128]{2,1,0:T(8,128)(2,1)S(1)}, u32[]{:S(2)}, u32[]{:S(2)}) async-start(bf16[32,136,128]{2,1,0:T(8,128)(2,1)} %gray.1), calls=%async_computation | async-start | bytes 2228224 | tf_op jit(solution)/shard_map/all_to_all | solution.py:366
  30.2 9.3 %collective-permute-start = (bf16[3,16,16,128]{3,2,1,0:T(8,128)(2,1)S(1)}, bf16[3,16,16,128]{3,2,1,0:T(8,128)(2,1)S(1)}, u32[]{:S(2)}, u32[]{:S(2)}) collective-permute-start(bf16[3,16,16,128]{3,2,1,0:T(8,128)(2,1)S(1)} %get-tuple-element.21), channel_id=1, source_target_pairs={{0,1},{2,3},{1,0},{3,2},{4,5},{6,7},{5,4},{7,6},{8,9},{10,11},{9,8... | collective-permute-start | bytes 589832 | tf_op jit(solution)/shard_map/ppermute | solution.py:388
  30.4 9.1 %collective-permute-start.1 = (bf16[3,16,16,128]{3,2,1,0:T(8,128)(2,1)S(1)}, bf16[3,16,16,128]{3,2,1,0:T(8,128)(2,1)S(1)}, u32[]{:S(2)}, u32[]{:S(2)}) collective-permute-start(bf16[3,16,16,128]{3,2,1,0:T(8,128)(2,1)S(1)} %get-tuple-element.22), channel_id=1, source_target_pairs={{1,2},{2,1},{5,6},{6,5},{9,10},{10,9},{13,14},{14,13},{17,18},{18,... | collective-permute-start | bytes 589832 | tf_op jit(solution)/shard_map/ppermute | solution.py:388

commit v6 on v5

--- a/solution.py
+++ b/solution.py
@@ -25,7 +25,7 @@
     return total
 
 
-PIECE = 4
+PIECE = 8
 
 
 def gray_kernel(chunks, weights_hbm, field_ref, out_ref, field, packed, weights_ref, arrived, sent, known):

time: 64.6 us -> 64.3 us (level)
  no operation moved by 1% of the time
where the time goes in v6:
time: 64.3 us; the launch traced here: 64 us
  blocking collectives  21.2 us (33%)
  waiting for transfers between devices  17.5 us (27%)
  starting transfers between devices  12.9 us (20%)
  Pallas kernels  12.3 us (19%)
    all_to_all x1, blocking collectives, per_device(): lax.all_to_all(depth.reshape(chunks, 128, LANES), group, 0, 0, tiled=True)  21.2 us
    all_to_all x1, waiting for transfers between devices, per_device(): lax.all_to_all(packed, group, 0, 0, tiled=True).reshape(8, 4, 136, LANES)  17.5 us
    all_to_all x1, starting transfers between devices, per_device(): lax.all_to_all(packed, group, 0, 0, tiled=True).reshape(8, 4, 136, LANES)  8.61 us
    pallas_call x1, Pallas kernels, per_device(): pl.pallas_call(inner_kernel, in_specs=[vmem, vmem, vmem], out_specs=[vmem...  5.05 us
    ppermute x2, starting transfers between devices, per_device(): lax.ppermute(rows, 'band', pairs + [(b, a) for a, b in pairs])  4.27 us
    pallas_call x1, Pallas kernels, per_device(): pl.pallas_call(functools.partial(gray_kernel, chunks), in_specs=[hbm, hbm...  3.32 us
    pallas_call x1, Pallas kernels, per_device(): pl.pallas_call(outer_kernel, in_specs=[vmem] * 5, out_specs=vmem, out_sha...  2.19 us
    pallas_call x1, Pallas kernels, per_device(): pl.pallas_call(functools.partial(spread_kernel, chunks), in_specs=[vmem],...  1.39 us
  transfers between devices with their start and end apart: 3, of which 1 were waited for; matrix products, arithmetic and copies ran while one was open for 0% of the time, Pallas kernels for 8%

profile of v6, /device:TPU:9, one launch (start us, length us, event | category | flops | bytes accessed | tf_op | source)
XLA Modules:
  0.0 64.0 jit_solution(28493647328351114)
XLA Ops:
  0.0 3.3 %gray.1 = bf16[32,136,128]{2,1,0:T(8,128)(2,1)} custom-call(f32[4]{0:T(128)} %weights_hbm.1, bf16[4,2,4,16,4096]{4,3,2,1,0:T(8,128)(2,1)} %field_ref.1), custom_call_target="tpu_custom_call" | custom-call | tf_op jit(solution)/shard_map/gray/pallas_call | solution.py:350
  3.3 8.6 %all-to-all-start = ((bf16[32,136,128]{2,1,0:T(8,128)(2,1)}), bf16[32,136,128]{2,1,0:T(8,128)(2,1)S(1)}, u32[]{:S(2)}, u32[]{:S(2)}) async-start(bf16[32,136,128]{2,1,0:T(8,128)(2,1)} %gray.1), calls=%async_computation | async-start | bytes 2228224 | tf_op jit(solution)/shard_map/all_to_all | solution.py:366
  12.0 0.1 matrices.1
  12.1 17.5 %all-to-all-done = bf16[32,136,128]{2,1,0:T(8,128)(2,1)S(1)} async-done(((bf16[32,136,128]{2,1,0:T(8,128)(2,1)}), bf16[32,136,128]{2,1,0:T(8,128)(2,1)S(1)}, u32[]{:S(2)}, u32[]{:S(2)}) %all-to-all-start) | async-done | bytes 1114144 | tf_op jit(solution)/shard_map/all_to_all | solution.py:366
  29.6 0.3 edges.1
  29.9 0.3 collective-permute-start
  30.1 4.0 %collective-permute-start.1 = (bf16[3,16,16,128]{3,2,1,0:T(8,128)(2,1)S(1)}, bf16[3,16,16,128]{3,2,1,0:T(8,128)(2,1)S(1)}, u32[]{:S(2)}, u32[]{:S(2)}) collective-permute-start(bf16[3,16,16,128]{3,2,1,0:T(8,128)(2,1)S(1)} %get-tuple-element.22), channel_id=1, source_target_pairs={{1,2},{2,1},{5,6},{6,5},{9,10},{10,9},{13,14},{14,13},{17,18},{18,... | collective-permute-start | bytes 589832 | tf_op jit(solution)/shard_map/ppermute | solution.py:388
  34.1 5.1 %inner.1 = (f32[3,16,272,128]{3,2,1,0:T(8,128)S(1)}, f32[16,16,16,128]{3,2,1,0:T(8,128)S(1)}, f32[16,272,128]{2,1,0:T(8,128)S(1)}) custom-call(bf16[8,4,136,128]{3,2,1,0:T(8,128)(2,1)S(1)} %bitcast.4, bf16[8,256,128]{2,1,0:T(8,128)(2,1)S(1)} %get-tuple-element.18.grads, bf16[8,256,128]{2,1,0:T(8,128)(2,1)S(1)} %get-tuple-element.19.smooths), custom_call_target="tpu_custom_call" | custom-call | flops 1000000000 | bytes 8388608 | tf_op jit(solution)/shard_map/inner/pallas_call | solution.py:392
  39.2 0.0 collective-permute-done.one_ref
  39.2 0.0 collective-permute-done.1.two_ref
  39.2 2.2 %outer.1 = bf16[8,4,2,64,128]{4,3,2,1,0:T(8,128)(2,1)S(1)} custom-call(f32[16,16,16,128]{3,2,1,0:T(8,128)S(1)} %get-tuple-element.20.gray_ref, bf16[3,16,16,128]{3,2,1,0:T(8,128)(2,1)S(1)} %collective-permute-done.one_ref, bf16[3,16,16,128]{3,2,1,0:T(8,128)(2,1)S(1)} %collective-permute-done.1.two_ref, f32[3,16,272,128]{3,2,1,0:T(8,128)S(1)} %get-tuple-element.23.hor_ref, ...), custom_call_target="tpu_custom_call" | custom-call | tf_op jit(solution)/shard_map/outer/pallas_call | solution.py:412
  41.4 21.2 %all_to_all.10.in_ref = bf16[32,128,128]{2,1,0:T(8,128)(2,1)S(1)} all-to-all(bf16[32,128,128]{2,1,0:T(8,128)(2,1)S(1)} %bitcast.5), channel_id=1, replica_groups=mesh['crow'=8,'ccol'=4,'band'=4] {'crow','ccol'}, dimensions={0} | all-to-all | bytes 2097152 | tf_op jit(solution)/shard_map/all_to_all | solution.py:426
  62.6 1.4 %spread.1 = f32[128,4096]{1,0:T(8,128)} custom-call(bf16[32,128,128]{2,1,0:T(8,128)(2,1)S(1)} %all_to_all.10.in_ref), custom_call_target="tpu_custom_call" | custom-call | tf_op jit(solution)/shard_map/spread/pallas_call | solution.py:427
Async XLA Ops:
  3.3 26.3 %all-to-all-start = ((bf16[32,136,128]{2,1,0:T(8,128)(2,1)}), bf16[32,136,128]{2,1,0:T(8,128)(2,1)S(1)}, u32[]{:S(2)}, u32[]{:S(2)}) async-start(bf16[32,136,128]{2,1,0:T(8,128)(2,1)} %gray.1), calls=%async_computation | async-start | bytes 2228224 | tf_op jit(solution)/shard_map/all_to_all | solution.py:366
  29.9 9.3 %collective-permute-start = (bf16[3,16,16,128]{3,2,1,0:T(8,128)(2,1)S(1)}, bf16[3,16,16,128]{3,2,1,0:T(8,128)(2,1)S(1)}, u32[]{:S(2)}, u32[]{:S(2)}) collective-permute-start(bf16[3,16,16,128]{3,2,1,0:T(8,128)(2,1)S(1)} %get-tuple-element.21), channel_id=1, source_target_pairs={{0,1},{2,3},{1,0},{3,2},{4,5},{6,7},{5,4},{7,6},{8,9},{10,11},{9,8... | collective-permute-start | bytes 589832 | tf_op jit(solution)/shard_map/ppermute | solution.py:388
  30.1 9.1 %collective-permute-start.1 = (bf16[3,16,16,128]{3,2,1,0:T(8,128)(2,1)S(1)}, bf16[3,16,16,128]{3,2,1,0:T(8,128)(2,1)S(1)}, u32[]{:S(2)}, u32[]{:S(2)}) collective-permute-start(bf16[3,16,16,128]{3,2,1,0:T(8,128)(2,1)S(1)} %get-tuple-element.22), channel_id=1, source_target_pairs={{1,2},{2,1},{5,6},{6,5},{9,10},{10,9},{13,14},{14,13},{17,18},{18,... | collective-permute-start | bytes 589832 | tf_op jit(solution)/shard_map/ppermute | solution.py:388
